TPU v7x, 32 devices: a whole 2x2x4 slice. The times are simulated.
32 devices in a mesh: row: 4 (over y, core), col: 8 (over z, x).
Axes of the slice: x: 2, y: 2, z: 4, core: 2. Of those that a mesh axis runs over, the one named last changes fastest.
Arguments:
- transition: bfloat16 [32768, 32768], P('row', 'col'), may hold values from 1.5258789e-06 to 0.0024414062, as said below
- emission: bfloat16 [96, 32768], P(None, 'col'), may hold values from 0.0099487305 to 1
- token_ids: int32 [2, 192], replicated, may hold values from 0 to 95
- forward: bfloat16 [2, 192, 32768], P(None, 'col', 'row'), may hold values from 3.0517578e-06 to 0.0008239746, as said below
- backward_last: float32 [192, 32768], P('row', 'col'), may hold values from 0.1 to 10
Outputs:
- backward: float32 [2, 192, 32768], P(None, 'col', 'row')
- counts: float32 [32768, 1024], P('row', 'col')
Inputs may be any that keep to these rules, and one draw needn't show every extreme that they name: Positive transition weights. Positive forward weights.
All inputs are finite; a program needn't handle non-finite values.
Results may differ from a plain program's by a relative error of at most 0.00048.
Values may be sent and summed in bfloat16 or wider, within the bound.
A program may use at most 192 MiB of HBM per device.

v0:
```python
import jax
import jax.numpy as jnp
from jax import lax
from jax.sharding import PartitionSpec as P

H = 32768
N = 192
DW = 128
CHUNKS = 2


def in_order(arrived, index):
    count = len(arrived)
    turned = jnp.stack([arrived[-i % count] for i in range(count)] * 2)
    return lax.dynamic_slice_in_dim(turned, (count - index) % count, count, 0)


def gather_small(value, col_count, col_index):
    arrived = [value]
    for k in range(1, col_count):
        arrived.append(lax.ppermute(value, "col", [(c, (c + k) % col_count) for c in range(col_count)]))
    place = lax.broadcasted_iota(jnp.int32, (col_count,) + value.shape, 0)
    out = jnp.zeros(place.shape, value.dtype)
    for k, got in enumerate(arrived):
        out = jnp.where(place == (col_index - k + col_count) % col_count, got[None], out)
    return out


def gather_rows(value, row_count, row_index):
    half = row_count // 2
    arrived = [value]
    for k in range(1, half):
        arrived.append(lax.ppermute(value, "row", [(r, (r + 2 * k) % row_count) for r in range(row_count)]))
    own = in_order(arrived, row_index // 2) if half > 1 else value[None]
    got = lax.ppermute(own, "row", [(r, r ^ 1) for r in range(row_count)])
    even = row_index % 2 == 0
    both = jnp.stack([jnp.where(even, own, got), jnp.where(even, got, own)], axis=1)
    return both.reshape(row_count * value.shape[0], value.shape[1])


def split_pair(partial, scale, col_count, col_index, local_seqs):
    scaled = (partial * scale).reshape(col_count // 2, 2, local_seqs, partial.shape[1])
    side = col_index % 2
    away = lax.dynamic_index_in_dim(scaled, 1 - side, 1, keepdims=False).astype(jnp.float16)
    return away, lax.dynamic_index_in_dim(scaled, side, 1, keepdims=False)


def reduce_scatter(away, keep, col_count, col_index):
    half = col_count // 2
    got = lax.ppermute(away, "col", [(c, c ^ 1) for c in range(col_count)])
    pair = keep + got.astype(jnp.float32)
    here = col_index // 2
    total = lax.dynamic_index_in_dim(pair, here, 0, keepdims=False)
    packed = pair.astype(jnp.float16)
    for k in range(1, half):
        piece = lax.dynamic_index_in_dim(packed, (here + k) % half, 0, keepdims=False)
        got = lax.ppermute(piece, "col", [(c, (c + 2 * k) % col_count) for c in range(col_count)])
        total = total + got.astype(jnp.float32)
    return total


def on_device(transition, emission, token_ids, forward, backward_last):
    row_count = lax.axis_size("row")
    col_count = lax.axis_size("col")
    row_index = lax.axis_index("row")
    col_index = lax.axis_index("col")
    ratio = col_count // row_count
    local_seqs = forward.shape[1]
    row_seqs = backward_last.shape[0]
    block_src = transition.shape[0]
    block_dst = transition.shape[1]
    seq_total = local_seqs * col_count
    columns = lax.broadcasted_iota(jnp.int32, (row_seqs, emission.shape[0]), 1)
    window = transition[:, :DW]
    outputs = [None, None]
    normals = [None, None]
    picked = [None, None]
    beta = backward_last
    scale = jnp.full((seq_total, 1), 64.0, jnp.float32)
    scale_mine = jnp.full((local_seqs, 1), 64.0, jnp.float32)
    chunk = block_src // CHUNKS
    for step in (1, 0):
        tokens = lax.dynamic_slice_in_dim(token_ids[step], row_index * row_seqs, row_seqs, 0)
        onehot = (tokens[:, None] == columns).astype(jnp.bfloat16)
        emitted = jnp.dot(onehot, emission, preferred_element_type=jnp.float32)
        local_back = (emitted * beta).astype(jnp.bfloat16)
        weighted_back = gather_rows(local_back, row_count, row_index)
        picked[step] = weighted_back[:, :DW]
        if step == 1:
            forward_all = lax.all_gather(forward, "col", axis=1, tiled=True)
        pieces = []
        for k in range(CHUNKS):
            rows = slice(k * chunk, (k + 1) * chunk)
            partial = lax.dot_general(
                weighted_back, transition[rows], (((1,), (1,)), ((), ())), preferred_element_type=jnp.float32
            )
            away, keep = split_pair(partial, scale, col_count, col_index, local_seqs)
            if k < CHUNKS - 1:
                weighted_back, away = lax.optimization_barrier((weighted_back, away))
            pieces.append(reduce_scatter(away, keep, col_count, col_index))
        mine = jnp.concatenate(pieces, axis=1) / scale_mine
        norm = jnp.sum(forward[step].astype(jnp.float32) * mine, axis=1)
        sums = lax.psum(jnp.stack([norm, jnp.sum(mine, axis=1)]), "row")
        sums_all = gather_small(sums, col_count, col_index)
        normals[step] = sums_all[:, 0].reshape(seq_total)
        outputs[step] = mine / sums[0][:, None]
        if step == 1:
            halves = outputs[step].reshape(local_seqs, ratio, block_dst)
            arrived = []
            for p in range(ratio):
                part = lax.dynamic_index_in_dim(halves, (col_index + p) % ratio, 1, keepdims=False)
                moves = []
                for r in range(row_count):
                    for c in range(col_count):
                        moves.append((r * col_count + c, (c // ratio) * col_count + r * ratio + (c + p) % ratio))
                arrived.append(lax.ppermute(part, ("row", "col"), moves))
            beta = in_order(arrived, col_index % ratio).reshape(row_seqs, block_dst)
            scale = (16777216.0 * sums_all[:, 0] / sums_all[:, 1]).reshape(seq_total, 1)
            scale_mine = (16777216.0 * sums[0] / sums[1])[:, None]
    totals = jnp.zeros((block_src, DW), jnp.float32)
    for step in (1, 0):
        scaled = (forward_all[step].astype(jnp.float32) / normals[step][:, None]).astype(jnp.bfloat16)
        totals = totals + lax.dot_general(
            scaled, picked[step], (((0,), (0,)), ((), ())), preferred_element_type=jnp.float32
        )
    counts = window.astype(jnp.float32) * totals * (H * H / N)
    return (jnp.stack(outputs), counts)


def solution(mesh):
    in_specs = (P("row", "col"), P(None, "col"), P(), P(None, "col", "row"), P("row", "col"))
    out_specs = (P(None, "col", "row"), P("row", "col"))
    return jax.shard_map(
        on_device, mesh=mesh, in_specs=in_specs, out_specs=out_specs, check_vma=False
    )
```

profile of v0, /device:TPU:0, one launch (start us, length us, event | category | flops | bytes accessed | tf_op | source)
XLA Modules:
  0.0 322.1 jit_solution(14443094737425642083)
XLA Ops:
  7.2 0.8 fusion.69
  8.1 0.3 copy-done
  8.3 1.4 fusion.24
  9.8 3.0 collective-permute-start
  12.8 9.1 %collective-permute-done = bf16[48,4096]{1,0:T(8,128)(2,1)S(1)} collective-permute-done((bf16[48,4096]{1,0:T(8,128)(2,1)S(1)}, bf16[48,4096]{1,0:T(8,128)(2,1)S(1)}, u32[]{:S(2)}, u32[]{:S(2)}) %collective-permute-start) | collective-permute-done | bytes 393248 | tf_op jit(solution)/shard_map/ppermute | solution.py:33
  21.9 0.5 fusion.41
  22.8 2.0 collective-permute-done.1
  24.8 0.6 select_bitcast_fusion.3
  25.8 18.2 %fusion.12 = f32[192,4096]{1,0:T(8,128)} fusion(bf16[192,4096]{1,0:T(8,128)(2,1)S(1)} %bitcast.158, bf16[8192,4096]{1,0:T(8,128)(2,1)} %param.5), kind=kOutput, calls=%fused_computation.15 | convolution fusion | flops 6443237376 | bytes 38273024 | tf_op jit(solution)/shard_map/dot_general | solution.py:94
  44.0 2.4 fusion.29
  46.4 1.7 collective-permute-start.2
  48.2 16.3 %fusion.18 = f32[192,4096]{1,0:T(8,128)S(1)} fusion(bf16[192,4096]{1,0:T(8,128)(2,1)S(1)} %bitcast.159, bf16[8192,4096]{1,0:T(8,128)(2,1)} %param.5), kind=kOutput, calls=%fused_computation.17 | convolution fusion | flops 6443237376 | bytes 38273024 | tf_op jit(solution)/shard_map/dot_general | solution.py:94
  64.5 0.3 collective-permute-start.6
  64.8 1.4 collective-permute-done.2
  66.2 2.0 fusion.67
  68.4 1.9 collective-permute-start.3
  70.3 2.5 collective-permute-start.4
  72.8 1.4 collective-permute-start.5
  74.2 25.9 %collective-permute-done.6 = f16[4,24,4096]{2,1,0:T(8,128)(2,1)S(1)} collective-permute-done((f16[4,24,4096]{2,1,0:T(8,128)(2,1)S(1)}, f16[4,24,4096]{2,1,0:T(8,128)(2,1)S(1)}, u32[]{:S(2)}, u32[]{:S(2)}) %collective-permute-start.6) | collective-permute-done | bytes 786464 | tf_op jit(solution)/shard_map/ppermute | solution.py:50
  100.1 0.3 fusion.68
  100.5 1.7 collective-permute-start.7
  102.2 2.7 collective-permute-start.8
  104.9 1.4 collective-permute-start.9
  106.3 8.0 %collective-permute-done.7 = f16[24,4096]{1,0:T(8,128)(2,1)S(1)} collective-permute-done((f16[24,4096]{1,0:T(8,128)(2,1)S(1)}, f16[24,4096]{1,0:T(8,128)(2,1)S(1)}, u32[]{:S(2)}, u32[]{:S(2)}) %collective-permute-start.7) | collective-permute-done | bytes 196640 | tf_op jit(solution)/shard_map/ppermute | solution.py:57
  114.3 18.2 %collective-permute-done.8 = f16[24,4096]{1,0:T(8,128)(2,1)S(1)} collective-permute-done((f16[24,4096]{1,0:T(8,128)(2,1)S(1)}, f16[24,4096]{1,0:T(8,128)(2,1)S(1)}, u32[]{:S(2)}, u32[]{:S(2)}) %collective-permute-start.8) | collective-permute-done | bytes 196640 | tf_op jit(solution)/shard_map/ppermute | solution.py:57
  132.6 0.3 fusion.45
  132.9 6.1 %psum.14 = f32[2,24]{1,0:T(2,128)S(1)} all-reduce(f32[2,24]{1,0:T(2,128)S(1)} %pad_maximum_fusion.3), channel_id=1, replica_groups=mesh['row'=4,'col'=8] {'row'}, use_global_device_ids=true, to_apply=%region_2.3 | all-reduce | flops 48 | bytes 384 | tf_op jit(solution)/shard_map/psum | solution.py:103
  139.2 0.7 collective-permute-start.10
  139.9 1.8 collective-permute-start.11
  141.8 21.1 %collective-permute-start.14 = (f32[2,24]{1,0:T(2,128)S(1)}, f32[2,24]{1,0:T(2,128)S(1)}, u32[]{:S(2)}, u32[]{:S(2)}) collective-permute-start(f32[2,24]{1,0:T(2,128)S(1)} %psum.14), channel_id=1, source_target_pairs={{0,7},{1,0},{2,1},{3,2},{4,3},{5,4},{6,5},{7,6},{8,15},{9,8},{10,9... | collective-permute-start | bytes 584 | tf_op jit(solution)/shard_map/ppermute | solution.py:21
  163.1 16.1 %collective-permute-start.17 = (f32[2,24]{1,0:T(2,128)S(1)}, f32[2,24]{1,0:T(2,128)S(1)}, u32[]{:S(2)}, u32[]{:S(2)}) collective-permute-start(f32[2,24]{1,0:T(2,128)S(1)} %psum.14), channel_id=1, source_target_pairs={{0,4},{1,5},{2,6},{3,7},{4,0},{5,1},{6,2},{7,3},{8,12},{9,13},{10,... | collective-permute-start | bytes 584 | tf_op jit(solution)/shard_map/ppermute | solution.py:21
  179.4 0.3 fusion.46
  179.7 11.1 %collective-permute-start.12 = (bf16[48,4096]{1,0:T(8,128)(2,1)S(1)}, bf16[48,4096]{1,0:T(8,128)(2,1)S(1)}, u32[]{:S(2)}, u32[]{:S(2)}) collective-permute-start(bf16[48,4096]{1,0:T(8,128)(2,1)S(1)} %fusion.46), channel_id=1, source_target_pairs={{0,16},{8,24},{16,0},{24,8},{1,17},{9,25},{17,1},{25,9},{2,18},{10... | collective-permute-start | bytes 1179656 | tf_op jit(solution)/shard_map/ppermute | solution.py:33
  190.8 1.0 fusion.43
  191.8 4.8 %collective-permute-done.12 = bf16[48,4096]{1,0:T(8,128)(2,1)S(1)} collective-permute-done((bf16[48,4096]{1,0:T(8,128)(2,1)S(1)}, bf16[48,4096]{1,0:T(8,128)(2,1)S(1)}, u32[]{:S(2)}, u32[]{:S(2)}) %collective-permute-start.12) | collective-permute-done | bytes 393248 | tf_op jit(solution)/shard_map/ppermute | solution.py:33
  196.5 0.5 fusion.35
  197.2 6.9 %collective-permute-start.18 = (f32[2,24]{1,0:T(2,128)S(1)}, f32[2,24]{1,0:T(2,128)S(1)}, u32[]{:S(2)}, u32[]{:S(2)}) collective-permute-start(f32[2,24]{1,0:T(2,128)S(1)} %psum.14), channel_id=1, source_target_pairs={{0,3},{1,4},{2,5},{3,6},{4,7},{5,0},{6,1},{7,2},{8,11},{9,12},{10,... | collective-permute-start | bytes 584 | tf_op jit(solution)/shard_map/ppermute | solution.py:21
  204.1 1.4 collective-permute-start.20
  205.5 3.9 %collective-permute-done.19 = f32[2,24]{1,0:T(2,128)S(1)} collective-permute-done((f32[2,24]{1,0:T(2,128)S(1)}, f32[2,24]{1,0:T(2,128)S(1)}, u32[]{:S(2)}, u32[]{:S(2)}) %collective-permute-start.19) | collective-permute-done | bytes 224 | tf_op jit(solution)/shard_map/ppermute | solution.py:21
  209.4 1.0 collective-permute-done.20
  210.8 0.6 select_bitcast_fusion.1
  211.7 17.1 %fusion.15 = f32[192,4096]{1,0:T(8,128)S(1)} fusion(bf16[192,4096]{1,0:T(8,128)(2,1)S(1)} %bitcast.161, bf16[8192,4096]{1,0:T(8,128)(2,1)} %param.5, f32[192]{0:T(256)S(1)} %multiply_divide_fusion), kind=kOutput, calls=%fused_computation.16 | convolution fusion | flops 6443237376 | bytes 38273792 | tf_op jit(solution)/shard_map/dot_general | solution.py:94
  228.7 1.0 fusion.31
  229.7 16.6 %fusion.21 = f32[192,4096]{1,0:T(8,128)S(1)} fusion(bf16[192,4096]{1,0:T(8,128)(2,1)} %bitcast.162, bf16[8192,4096]{1,0:T(8,128)(2,1)} %param.5, f32[192]{0:T(256)S(1)} %multiply_divide_fusion), kind=kOutput, calls=%fused_computation.18 | convolution fusion | flops 6443237376 | bytes 38273792 | tf_op jit(solution)/shard_map/dot_general | solution.py:94
  246.5 2.1 collective-permute-start.25
  248.8 1.4 fusion.65
  250.4 2.3 collective-permute-start.23
  252.7 1.5 collective-permute-start.24
  254.2 11.1 %collective-permute-done.25 = f16[4,24,4096]{2,1,0:T(8,128)(2,1)S(1)} collective-permute-done((f16[4,24,4096]{2,1,0:T(8,128)(2,1)S(1)}, f16[4,24,4096]{2,1,0:T(8,128)(2,1)S(1)}, u32[]{:S(2)}, u32[]{:S(2)}) %collective-permute-start.25) | collective-permute-done | bytes 786464 | tf_op jit(solution)/shard_map/ppermute | solution.py:50
  265.3 0.3 fusion.66
  265.8 2.2 collective-permute-start.27
  268.0 1.6 collective-permute-start.28
  269.7 5.8 %collective-permute-done.26 = f16[24,4096]{1,0:T(8,128)(2,1)S(1)} collective-permute-done((f16[24,4096]{1,0:T(8,128)(2,1)S(1)}, f16[24,4096]{1,0:T(8,128)(2,1)S(1)}, u32[]{:S(2)}, u32[]{:S(2)}) %collective-permute-start.26) | collective-permute-done | bytes 196640 | tf_op jit(solution)/shard_map/ppermute | solution.py:57
  275.4 7.4 %collective-permute-done.27 = f16[24,4096]{1,0:T(8,128)(2,1)S(1)} collective-permute-done((f16[24,4096]{1,0:T(8,128)(2,1)S(1)}, f16[24,4096]{1,0:T(8,128)(2,1)S(1)}, u32[]{:S(2)}, u32[]{:S(2)}) %collective-permute-start.27) | collective-permute-done | bytes 196640 | tf_op jit(solution)/shard_map/ppermute | solution.py:57
  282.9 0.4 fusion.44
  283.3 5.7 %psum.15 = f32[2,24]{1,0:T(2,128)S(1)} all-reduce(f32[2,24]{1,0:T(2,128)S(1)} %pad_maximum_fusion.4), channel_id=1, replica_groups=mesh['row'=4,'col'=8] {'row'}, use_global_device_ids=true, to_apply=%region_5.6 | all-reduce | flops 48 | bytes 384 | tf_op jit(solution)/shard_map/psum | solution.py:103
  289.0 4.8 %collective-permute-start.34 = (f32[2,24]{1,0:T(2,128)S(1)}, f32[2,24]{1,0:T(2,128)S(1)}, u32[]{:S(2)}, u32[]{:S(2)}) collective-permute-start(f32[2,24]{1,0:T(2,128)S(1)} %psum.15), channel_id=1, source_target_pairs={{0,2},{1,3},{2,4},{3,5},{4,6},{5,7},{6,0},{7,1},{8,10},{9,11},{10,... | collective-permute-start | bytes 584 | tf_op jit(solution)/shard_map/ppermute | solution.py:21
  293.8 4.7 %collective-permute-start.32 = (f32[2,24]{1,0:T(2,128)S(1)}, f32[2,24]{1,0:T(2,128)S(1)}, u32[]{:S(2)}, u32[]{:S(2)}) collective-permute-start(f32[2,24]{1,0:T(2,128)S(1)} %psum.15), channel_id=1, source_target_pairs={{0,4},{1,5},{2,6},{3,7},{4,0},{5,1},{6,2},{7,3},{8,12},{9,13},{10,... | collective-permute-start | bytes 584 | tf_op jit(solution)/shard_map/ppermute | solution.py:21
  298.7 1.3 pad_maximum_fusion.2
  300.0 2.4 collective-permute-start.30
  302.3 1.5 collective-permute-start.29
  303.9 2.1 collective-permute-done.29
  306.2 3.5 %fusion.27 = f32[8192,128]{1,0:T(8,128)S(1)} fusion(bf16[2,192,8192]{2,1,0:T(8,128)(2,1)} %all-gather.2.cloned.1.call-done, f32[192]{0:T(256)S(1)} %squeeze.102, bf16[192,4096]{1,0:T(8,128)(2,1)} %bitcast.160), kind=kOutput, calls=%fused_computation.24 | convolution fusion | flops 407371776 | bytes 7389952 | tf_op jit(solution)/shard_map/dot_general | solution.py:123
  310.0 5.3 %fusion.9 = f32[8192,128]{1,0:T(8,128)} fusion(f32[8192,128]{1,0:T(8,128)S(1)} %fusion.27, bf16[2,192,8192]{2,1,0:T(8,128)(2,1)S(1)} %copy-done.7, f32[192]{0:T(256)S(1)} %div.129, bf16[8192,4096]{1,0:T(8,128)(2,1)} %param.5, bf16[192,4096]{1,0:T(8,128)(2,1)} %bitcast.163), kind=kOutput, calls=%fused_computation.10 | convolution fusion | flops 411566080 | bytes 13681664 | tf_op jit(solution)/shard_map/dot_general | solution.py:123
  (95 shorter events, 4.0 us)
Async XLA Ops:
  7.2 1.2 copy-start
  7.2 299.0 %all-gather.2.cloned.1.call-start = ((), (), s32[]{:S(2)}) async-start(), calls=%async_computation | async-start | bytes 7077888 | tf_op jit(solution)/shard_map/all_gather | solution.py:90
  9.8 12.1 %collective-permute-start = (bf16[48,4096]{1,0:T(8,128)(2,1)S(1)}, bf16[48,4096]{1,0:T(8,128)(2,1)S(1)}, u32[]{:S(2)}, u32[]{:S(2)}) collective-permute-start(bf16[48,4096]{1,0:T(8,128)(2,1)S(1)} %fusion.24), channel_id=1, source_target_pairs={{0,16},{8,24},{16,0},{24,8},{1,17},{9,25},{17,1},{25,9},{2,18},{10... | collective-permute-start | bytes 1179656 | tf_op jit(solution)/shard_map/ppermute | solution.py:33
  22.5 2.4 collective-permute-start.1
  25.8 22.4 %copy-start.5 = (bf16[2,2,48,4096]{3,2,1,0:T(8,128)(2,1)}, bf16[2,2,48,4096]{3,2,1,0:T(8,128)(2,1)S(1)}, u32[]{:S(2)}) copy-start(bf16[2,2,48,4096]{3,2,1,0:T(8,128)(2,1)S(1)} %copy.7) | copy-start | bytes 4718596
  46.4 19.8 %collective-permute-start.2 = (f16[4,24,4096]{2,1,0:T(8,128)(2,1)}, f16[4,24,4096]{2,1,0:T(8,128)(2,1)S(1)}, u32[]{:S(2)}, u32[]{:S(2)}) collective-permute-start(f16[4,24,4096]{2,1,0:T(8,128)(2,1)} %fusion.29), channel_id=1, source_target_pairs={{0,1},{1,0},{2,3},{3,2},{4,5},{5,4},{6,7},{7,6},{8,9},{9,8},{10,11... | collective-permute-start | bytes 2359304 | tf_op jit(solution)/shard_map/ppermute | solution.py:50
  64.5 35.6 %collective-permute-start.6 = (f16[4,24,4096]{2,1,0:T(8,128)(2,1)S(1)}, f16[4,24,4096]{2,1,0:T(8,128)(2,1)S(1)}, u32[]{:S(2)}, u32[]{:S(2)}) collective-permute-start(f16[4,24,4096]{2,1,0:T(8,128)(2,1)S(1)} %fusion.30), channel_id=1, source_target_pairs={{0,1},{1,0},{2,3},{3,2},{4,5},{5,4},{6,7},{7,6},{8,9},{9,8},{10,11... | collective-permute-start | bytes 2359304 | tf_op jit(solution)/shard_map/ppermute | solution.py:50
  68.4 36.5 %collective-permute-start.3 = (f16[24,4096]{1,0:T(8,128)(2,1)S(1)}, f16[24,4096]{1,0:T(8,128)(2,1)S(1)}, u32[]{:S(2)}, u32[]{:S(2)}) collective-permute-start(f16[24,4096]{1,0:T(8,128)(2,1)S(1)} %get-tuple-element.36), channel_id=1, source_target_pairs={{0,2},{1,3},{2,4},{3,5},{4,6},{5,7},{6,0},{7,1},{8,10},{9,11},{10,... | collective-permute-start | bytes 589832 | tf_op jit(solution)/shard_map/ppermute | solution.py:57
  70.3 36.0 %collective-permute-start.4 = (f16[24,4096]{1,0:T(8,128)(2,1)S(1)}, f16[24,4096]{1,0:T(8,128)(2,1)S(1)}, u32[]{:S(2)}, u32[]{:S(2)}) collective-permute-start(f16[24,4096]{1,0:T(8,128)(2,1)S(1)} %get-tuple-element.38), channel_id=1, source_target_pairs={{0,4},{1,5},{2,6},{3,7},{4,0},{5,1},{6,2},{7,3},{8,12},{9,13},{10,... | collective-permute-start | bytes 589832 | tf_op jit(solution)/shard_map/ppermute | solution.py:57
  72.8 33.5 %collective-permute-start.5 = (f16[24,4096]{1,0:T(8,128)(2,1)S(1)}, f16[24,4096]{1,0:T(8,128)(2,1)S(1)}, u32[]{:S(2)}, u32[]{:S(2)}) collective-permute-start(f16[24,4096]{1,0:T(8,128)(2,1)S(1)} %get-tuple-element.37), channel_id=1, source_target_pairs={{0,6},{1,7},{2,0},{3,1},{4,2},{5,3},{6,4},{7,5},{8,14},{9,15},{10,... | collective-permute-start | bytes 589832 | tf_op jit(solution)/shard_map/ppermute | solution.py:57
  100.5 32.1 %copy-start.2 = (bf16[2,24,8192]{2,1,0:T(8,128)(2,1)S(1)}, bf16[2,24,8192]{2,1,0:T(8,128)(2,1)}, u32[]{:S(2)}) copy-start(bf16[2,24,8192]{2,1,0:T(8,128)(2,1)} %param.8) | copy-start | bytes 2359300
  100.5 13.8 %collective-permute-start.7 = (f16[24,4096]{1,0:T(8,128)(2,1)S(1)}, f16[24,4096]{1,0:T(8,128)(2,1)S(1)}, u32[]{:S(2)}, u32[]{:S(2)}) collective-permute-start(f16[24,4096]{1,0:T(8,128)(2,1)S(1)} %get-tuple-element.39), channel_id=1, source_target_pairs={{0,2},{1,3},{2,4},{3,5},{4,6},{5,7},{6,0},{7,1},{8,10},{9,11},{10,... | collective-permute-start | bytes 589832 | tf_op jit(solution)/shard_map/ppermute | solution.py:57
  102.2 30.3 %collective-permute-start.8 = (f16[24,4096]{1,0:T(8,128)(2,1)S(1)}, f16[24,4096]{1,0:T(8,128)(2,1)S(1)}, u32[]{:S(2)}, u32[]{:S(2)}) collective-permute-start(f16[24,4096]{1,0:T(8,128)(2,1)S(1)} %get-tuple-element.41), channel_id=1, source_target_pairs={{0,4},{1,5},{2,6},{3,7},{4,0},{5,1},{6,2},{7,3},{8,12},{9,13},{10,... | collective-permute-start | bytes 589832 | tf_op jit(solution)/shard_map/ppermute | solution.py:57
  104.9 27.6 %collective-permute-start.9 = (f16[24,4096]{1,0:T(8,128)(2,1)S(1)}, f16[24,4096]{1,0:T(8,128)(2,1)S(1)}, u32[]{:S(2)}, u32[]{:S(2)}) collective-permute-start(f16[24,4096]{1,0:T(8,128)(2,1)S(1)} %get-tuple-element.40), channel_id=1, source_target_pairs={{0,6},{1,7},{2,0},{3,1},{4,2},{5,3},{6,4},{7,5},{8,14},{9,15},{10,... | collective-permute-start | bytes 589832 | tf_op jit(solution)/shard_map/ppermute | solution.py:57
  139.2 23.9 %collective-permute-start.10 = (f32[24,4096]{1,0:T(8,128)S(1)}, f32[24,4096]{1,0:T(8,128)S(1)}, u32[]{:S(2)}, u32[]{:S(2)}) collective-permute-start(f32[24,4096]{1,0:T(8,128)S(1)} %get-tuple-element.35), channel_id=1, source_target_pairs={{0,0},{1,1},{2,8},{3,9},{4,16},{5,17},{6,24},{7,25},{8,2},{9,3},{1... | collective-permute-start | bytes 1179656 | tf_op jit(solution)/shard_map/ppermute | solution.py:116
  139.9 39.3 %collective-permute-start.11 = (f32[24,4096]{1,0:T(8,128)S(1)}, f32[24,4096]{1,0:T(8,128)S(1)}, u32[]{:S(2)}, u32[]{:S(2)}) collective-permute-start(f32[24,4096]{1,0:T(8,128)S(1)} %get-tuple-element.34), channel_id=1, source_target_pairs={{0,1},{1,0},{2,9},{3,8},{4,17},{5,16},{6,25},{7,24},{8,3},{9,2},{1... | collective-permute-start | bytes 1179656 | tf_op jit(solution)/shard_map/ppermute | solution.py:116
  141.8 55.4 %collective-permute-start.14 = (f32[2,24]{1,0:T(2,128)S(1)}, f32[2,24]{1,0:T(2,128)S(1)}, u32[]{:S(2)}, u32[]{:S(2)}) collective-permute-start(f32[2,24]{1,0:T(2,128)S(1)} %psum.14), channel_id=1, source_target_pairs={{0,7},{1,0},{2,1},{3,2},{4,3},{5,4},{6,5},{7,6},{8,15},{9,8},{10,9... | collective-permute-start | bytes 584 | tf_op jit(solution)/shard_map/ppermute | solution.py:21
  162.9 41.2 %collective-permute-start.15 = (f32[2,24]{1,0:T(2,128)S(1)}, f32[2,24]{1,0:T(2,128)S(1)}, u32[]{:S(2)}, u32[]{:S(2)}) collective-permute-start(f32[2,24]{1,0:T(2,128)S(1)} %psum.14), channel_id=1, source_target_pairs={{0,6},{1,7},{2,0},{3,1},{4,2},{5,3},{6,4},{7,5},{8,14},{9,15},{10,... | collective-permute-start | bytes 584 | tf_op jit(solution)/shard_map/ppermute | solution.py:21
  163.1 41.0 %collective-permute-start.16 = (f32[2,24]{1,0:T(2,128)S(1)}, f32[2,24]{1,0:T(2,128)S(1)}, u32[]{:S(2)}, u32[]{:S(2)}) collective-permute-start(f32[2,24]{1,0:T(2,128)S(1)} %psum.14), channel_id=1, source_target_pairs={{0,5},{1,6},{2,7},{3,0},{4,1},{5,2},{6,3},{7,4},{8,13},{9,14},{10,... | collective-permute-start | bytes 584 | tf_op jit(solution)/shard_map/ppermute | solution.py:21
  163.1 42.4 %collective-permute-start.17 = (f32[2,24]{1,0:T(2,128)S(1)}, f32[2,24]{1,0:T(2,128)S(1)}, u32[]{:S(2)}, u32[]{:S(2)}) collective-permute-start(f32[2,24]{1,0:T(2,128)S(1)} %psum.14), channel_id=1, source_target_pairs={{0,4},{1,5},{2,6},{3,7},{4,0},{5,1},{6,2},{7,3},{8,12},{9,13},{10,... | collective-permute-start | bytes 584 | tf_op jit(solution)/shard_map/ppermute | solution.py:21
  179.7 16.8 %collective-permute-start.12 = (bf16[48,4096]{1,0:T(8,128)(2,1)S(1)}, bf16[48,4096]{1,0:T(8,128)(2,1)S(1)}, u32[]{:S(2)}, u32[]{:S(2)}) collective-permute-start(bf16[48,4096]{1,0:T(8,128)(2,1)S(1)} %fusion.46), channel_id=1, source_target_pairs={{0,16},{8,24},{16,0},{24,8},{1,17},{9,25},{17,1},{25,9},{2,18},{10... | collective-permute-start | bytes 1179656 | tf_op jit(solution)/shard_map/ppermute | solution.py:33
  197.1 13.7 %collective-permute-start.13 = (bf16[2,48,4096]{2,1,0:T(8,128)(2,1)S(1)}, bf16[2,48,4096]{2,1,0:T(8,128)(2,1)S(1)}, u32[]{:S(2)}, u32[]{:S(2)}) collective-permute-start(bf16[2,48,4096]{2,1,0:T(8,128)(2,1)S(1)} %fusion.35), channel_id=1, source_target_pairs={{0,8},{8,0},{16,24},{24,16},{1,9},{9,1},{17,25},{25,17},{2,10},{10... | collective-permute-start | bytes 2359304 | tf_op jit(solution)/shard_map/ppermute | solution.py:35
  197.2 8.3 %collective-permute-start.18 = (f32[2,24]{1,0:T(2,128)S(1)}, f32[2,24]{1,0:T(2,128)S(1)}, u32[]{:S(2)}, u32[]{:S(2)}) collective-permute-start(f32[2,24]{1,0:T(2,128)S(1)} %psum.14), channel_id=1, source_target_pairs={{0,3},{1,4},{2,5},{3,6},{4,7},{5,0},{6,1},{7,2},{8,11},{9,12},{10,... | collective-permute-start | bytes 584 | tf_op jit(solution)/shard_map/ppermute | solution.py:21
  204.1 5.4 %collective-permute-start.19 = (f32[2,24]{1,0:T(2,128)S(1)}, f32[2,24]{1,0:T(2,128)S(1)}, u32[]{:S(2)}, u32[]{:S(2)}) collective-permute-start(f32[2,24]{1,0:T(2,128)S(1)} %psum.14), channel_id=1, source_target_pairs={{0,2},{1,3},{2,4},{3,5},{4,6},{5,7},{6,0},{7,1},{8,10},{9,11},{10,... | collective-permute-start | bytes 584 | tf_op jit(solution)/shard_map/ppermute | solution.py:21
  204.1 6.3 %collective-permute-start.20 = (f32[2,24]{1,0:T(2,128)S(1)}, f32[2,24]{1,0:T(2,128)S(1)}, u32[]{:S(2)}, u32[]{:S(2)}) collective-permute-start(f32[2,24]{1,0:T(2,128)S(1)} %psum.14), channel_id=1, source_target_pairs={{0,1},{1,2},{2,3},{3,4},{4,5},{5,6},{6,7},{7,0},{8,9},{9,10},{10,1... | collective-permute-start | bytes 584 | tf_op jit(solution)/shard_map/ppermute | solution.py:21
  211.7 17.1 %copy-start.6 = (bf16[2,2,48,4096]{3,2,1,0:T(8,128)(2,1)}, bf16[2,2,48,4096]{3,2,1,0:T(8,128)(2,1)S(1)}, u32[]{:S(2)}) copy-start(bf16[2,2,48,4096]{3,2,1,0:T(8,128)(2,1)S(1)} %copy.8) | copy-start | bytes 4718596
  229.7 19.0 %collective-permute-start.21 = (f16[4,24,4096]{2,1,0:T(8,128)(2,1)}, f16[4,24,4096]{2,1,0:T(8,128)(2,1)}, u32[]{:S(2)}, u32[]{:S(2)}) collective-permute-start(f16[4,24,4096]{2,1,0:T(8,128)(2,1)} %fusion.31), channel_id=1, source_target_pairs={{0,1},{1,0},{2,3},{3,2},{4,5},{5,4},{6,7},{7,6},{8,9},{9,8},{10,11... | collective-permute-start | bytes 2359304 | tf_op jit(solution)/shard_map/ppermute | solution.py:50
  246.5 18.8 %collective-permute-start.25 = (f16[4,24,4096]{2,1,0:T(8,128)(2,1)S(1)}, f16[4,24,4096]{2,1,0:T(8,128)(2,1)S(1)}, u32[]{:S(2)}, u32[]{:S(2)}) collective-permute-start(f16[4,24,4096]{2,1,0:T(8,128)(2,1)S(1)} %fusion.32), channel_id=1, source_target_pairs={{0,1},{1,0},{2,3},{3,2},{4,5},{5,4},{6,7},{7,6},{8,9},{9,8},{10,11... | collective-permute-start | bytes 2359304 | tf_op jit(solution)/shard_map/ppermute | solution.py:50
  250.3 17.7 %collective-permute-start.22 = (f16[24,4096]{1,0:T(8,128)(2,1)S(1)}, f16[24,4096]{1,0:T(8,128)(2,1)S(1)}, u32[]{:S(2)}, u32[]{:S(2)}) collective-permute-start(f16[24,4096]{1,0:T(8,128)(2,1)S(1)} %get-tuple-element.28), channel_id=1, source_target_pairs={{0,2},{1,3},{2,4},{3,5},{4,6},{5,7},{6,0},{7,1},{8,10},{9,11},{10,... | collective-permute-start | bytes 589832 | tf_op jit(solution)/shard_map/ppermute | solution.py:57
  250.4 19.2 %collective-permute-start.23 = (f16[24,4096]{1,0:T(8,128)(2,1)S(1)}, f16[24,4096]{1,0:T(8,128)(2,1)S(1)}, u32[]{:S(2)}, u32[]{:S(2)}) collective-permute-start(f16[24,4096]{1,0:T(8,128)(2,1)S(1)} %get-tuple-element.30), channel_id=1, source_target_pairs={{0,4},{1,5},{2,6},{3,7},{4,0},{5,1},{6,2},{7,3},{8,12},{9,13},{10,... | collective-permute-start | bytes 589832 | tf_op jit(solution)/shard_map/ppermute | solution.py:57
  252.7 16.9 %collective-permute-start.24 = (f16[24,4096]{1,0:T(8,128)(2,1)S(1)}, f16[24,4096]{1,0:T(8,128)(2,1)S(1)}, u32[]{:S(2)}, u32[]{:S(2)}) collective-permute-start(f16[24,4096]{1,0:T(8,128)(2,1)S(1)} %get-tuple-element.29), channel_id=1, source_target_pairs={{0,6},{1,7},{2,0},{3,1},{4,2},{5,3},{6,4},{7,5},{8,14},{9,15},{10,... | collective-permute-start | bytes 589832 | tf_op jit(solution)/shard_map/ppermute | solution.py:57
  265.7 17.2 %copy-start.3 = (bf16[2,24,8192]{2,1,0:T(8,128)(2,1)S(1)}, bf16[2,24,8192]{2,1,0:T(8,128)(2,1)}, u32[]{:S(2)}) copy-start(bf16[2,24,8192]{2,1,0:T(8,128)(2,1)} %param.8) | copy-start | bytes 2359300
  265.7 9.7 %collective-permute-start.26 = (f16[24,4096]{1,0:T(8,128)(2,1)S(1)}, f16[24,4096]{1,0:T(8,128)(2,1)S(1)}, u32[]{:S(2)}, u32[]{:S(2)}) collective-permute-start(f16[24,4096]{1,0:T(8,128)(2,1)S(1)} %get-tuple-element.31), channel_id=1, source_target_pairs={{0,2},{1,3},{2,4},{3,5},{4,6},{5,7},{6,0},{7,1},{8,10},{9,11},{10,... | collective-permute-start | bytes 589832 | tf_op jit(solution)/shard_map/ppermute | solution.py:57
  265.8 17.0 %collective-permute-start.27 = (f16[24,4096]{1,0:T(8,128)(2,1)S(1)}, f16[24,4096]{1,0:T(8,128)(2,1)S(1)}, u32[]{:S(2)}, u32[]{:S(2)}) collective-permute-start(f16[24,4096]{1,0:T(8,128)(2,1)S(1)} %get-tuple-element.33), channel_id=1, source_target_pairs={{0,4},{1,5},{2,6},{3,7},{4,0},{5,1},{6,2},{7,3},{8,12},{9,13},{10,... | collective-permute-start | bytes 589832 | tf_op jit(solution)/shard_map/ppermute | solution.py:57
  268.0 14.8 %collective-permute-start.28 = (f16[24,4096]{1,0:T(8,128)(2,1)S(1)}, f16[24,4096]{1,0:T(8,128)(2,1)S(1)}, u32[]{:S(2)}, u32[]{:S(2)}) collective-permute-start(f16[24,4096]{1,0:T(8,128)(2,1)S(1)} %get-tuple-element.32), channel_id=1, source_target_pairs={{0,6},{1,7},{2,0},{3,1},{4,2},{5,3},{6,4},{7,5},{8,14},{9,15},{10,... | collective-permute-start | bytes 589832 | tf_op jit(solution)/shard_map/ppermute | solution.py:57
  282.9 15.8 %copy-start.4 = (f32[1,24,8192]{2,1,0:T(8,128)S(1)}, f32[1,24,8192]{2,1,0:T(8,128)}, u32[]{:S(2)}) copy-start(f32[1,24,8192]{2,1,0:T(8,128)} %fusion.43) | copy-start | bytes 2359300
  289.0 16.9 %collective-permute-start.35 = (f32[2,24]{1,0:T(2,128)S(1)}, f32[2,24]{1,0:T(2,128)S(1)}, u32[]{:S(2)}, u32[]{:S(2)}) collective-permute-start(f32[2,24]{1,0:T(2,128)S(1)} %psum.15), channel_id=1, source_target_pairs={{0,1},{1,2},{2,3},{3,4},{4,5},{5,6},{6,7},{7,0},{8,9},{9,10},{10,1... | collective-permute-start | bytes 584 | tf_op jit(solution)/shard_map/ppermute | solution.py:21
  289.0 10.9 %collective-permute-start.34 = (f32[2,24]{1,0:T(2,128)S(1)}, f32[2,24]{1,0:T(2,128)S(1)}, u32[]{:S(2)}, u32[]{:S(2)}) collective-permute-start(f32[2,24]{1,0:T(2,128)S(1)} %psum.15), channel_id=1, source_target_pairs={{0,2},{1,3},{2,4},{3,5},{4,6},{5,7},{6,0},{7,1},{8,10},{9,11},{10,... | collective-permute-start | bytes 584 | tf_op jit(solution)/shard_map/ppermute | solution.py:21
  293.8 8.5 %collective-permute-start.33 = (f32[2,24]{1,0:T(2,128)S(1)}, f32[2,24]{1,0:T(2,128)S(1)}, u32[]{:S(2)}, u32[]{:S(2)}) collective-permute-start(f32[2,24]{1,0:T(2,128)S(1)} %psum.15), channel_id=1, source_target_pairs={{0,3},{1,4},{2,5},{3,6},{4,7},{5,0},{6,1},{7,2},{8,11},{9,12},{10,... | collective-permute-start | bytes 584 | tf_op jit(solution)/shard_map/ppermute | solution.py:21
  293.8 10.0 %collective-permute-start.32 = (f32[2,24]{1,0:T(2,128)S(1)}, f32[2,24]{1,0:T(2,128)S(1)}, u32[]{:S(2)}, u32[]{:S(2)}) collective-permute-start(f32[2,24]{1,0:T(2,128)S(1)} %psum.15), channel_id=1, source_target_pairs={{0,4},{1,5},{2,6},{3,7},{4,0},{5,1},{6,2},{7,3},{8,12},{9,13},{10,... | collective-permute-start | bytes 584 | tf_op jit(solution)/shard_map/ppermute | solution.py:21
  298.6 5.3 %collective-permute-start.31 = (f32[2,24]{1,0:T(2,128)S(1)}, f32[2,24]{1,0:T(2,128)S(1)}, u32[]{:S(2)}, u32[]{:S(2)}) collective-permute-start(f32[2,24]{1,0:T(2,128)S(1)} %psum.15), channel_id=1, source_target_pairs={{0,5},{1,6},{2,7},{3,0},{4,1},{5,2},{6,3},{7,4},{8,13},{9,14},{10,... | collective-permute-start | bytes 584 | tf_op jit(solution)/shard_map/ppermute | solution.py:21
  300.0 3.9 %collective-permute-start.30 = (f32[2,24]{1,0:T(2,128)S(1)}, f32[2,24]{1,0:T(2,128)S(1)}, u32[]{:S(2)}, u32[]{:S(2)}) collective-permute-start(f32[2,24]{1,0:T(2,128)S(1)} %psum.15), channel_id=1, source_target_pairs={{0,6},{1,7},{2,0},{3,1},{4,2},{5,3},{6,4},{7,5},{8,14},{9,15},{10,... | collective-permute-start | bytes 584 | tf_op jit(solution)/shard_map/ppermute | solution.py:21
  302.3 3.6 %collective-permute-start.29 = (f32[2,24]{1,0:T(2,128)S(1)}, f32[2,24]{1,0:T(2,128)S(1)}, u32[]{:S(2)}, u32[]{:S(2)}) collective-permute-start(f32[2,24]{1,0:T(2,128)S(1)} %psum.15), channel_id=1, source_target_pairs={{0,7},{1,0},{2,1},{3,2},{4,3},{5,4},{6,5},{7,6},{8,15},{9,8},{10,9... | collective-permute-start | bytes 584 | tf_op jit(solution)/shard_map/ppermute | solution.py:21
  306.2 3.8 %copy-start.7 = (bf16[2,192,8192]{2,1,0:T(8,128)(2,1)S(1)}, bf16[2,192,8192]{2,1,0:T(8,128)(2,1)}, u32[]{:S(2)}) copy-start(bf16[2,192,8192]{2,1,0:T(8,128)(2,1)} %all-gather.2.cloned.1.call-done) | copy-start | bytes 18874372
  310.0 5.3 %copy-start.1 = (bf16[96,4096]{1,0:T(8,128)(2,1)S(1)}, bf16[96,4096]{1,0:T(8,128)(2,1)}, u32[]{:S(2)}) copy-start(bf16[96,4096]{1,0:T(8,128)(2,1)} %param.6) | copy-start | bytes 2359300
Sparse Core Ops, SparseCore 0:
  22.7 131.6 all-gather.1
where the time goes:
time: 323 us; the launch traced here: 322 us
  waiting for transfers between devices  101 us (31%)
  starting transfers between devices  99.3 us (31%)
  matrix products  78.8 us (24%)
  between operations  14.8 us (5%)
  other arithmetic  14.3 us (4%)
  blocking collectives  11.7 us (4%)
    dot_general x4, matrix products, on_device(): lax.dot_general(weighted_back, transition[rows], (((1,), (1,)), ((), ()))...  68.2 us
    ppermute x14, starting transfers between devices, gather_small(): lax.ppermute(value, 'col', [(c, (c + k) % col_count) for c in range(col_c...  59.1 us
    ppermute x12, waiting for transfers between devices, reduce_scatter(): lax.ppermute(piece, 'col', [(c, (c + 2 * k) % col_count) for c in range(c...  39.3 us
    ppermute x4, waiting for transfers between devices, reduce_scatter(): got = lax.ppermute(away, 'col', [(c, c ^ 1) for c in range(col_count)])  38.7 us
    ppermute x12, starting transfers between devices, reduce_scatter(): lax.ppermute(piece, 'col', [(c, (c + 2 * k) % col_count) for c in range(c...  19.2 us
    ppermute x2, starting transfers between devices, gather_rows(): lax.ppermute(value, 'row', [(r, (r + 2 * k) % row_count) for r in range(r...  14.1 us
    ppermute x2, waiting for transfers between devices, gather_rows(): lax.ppermute(value, 'row', [(r, (r + 2 * k) % row_count) for r in range(r...  13.9 us
    psum x2, blocking collectives, on_device(): sums = lax.psum(jnp.stack([norm, jnp.sum(mine, axis=1)]), 'row')  11.7 us
  transfers between devices with their start and end apart: 37, of which 14 were waited for; matrix products, arithmetic and copies ran while one was open for 26% of the time, Pallas kernels for 0%

commit v1 on v0

--- a/solution.py
+++ b/solution.py
@@ -1,12 +1,154 @@
+import functools
+import math
+
 import jax
 import jax.numpy as jnp
 from jax import lax
+from jax.experimental import pallas as pl
+from jax.experimental.pallas import tpu as pltpu
 from jax.sharding import PartitionSpec as P
 
 H = 32768
 N = 192
 DW = 128
 CHUNKS = 2
+A_MIN, A_MAX = 1.5258789e-06, 0.0024414062
+E_MIN, E_MAX = 0.0099487305, 1.0
+B_MIN, B_MAX = 0.1, 10.0
+F_MIN, F_MAX = 3.0517578e-06, 0.0008239746
+CHUNK = 1024
+SLOTS = 4
+MESH = pl.DeviceIdType.MESH
+
+
+def code_range(lo, hi):
+    low = math.log2(lo) - 0.5
+    high = math.log2(hi) + 0.5
+    return 65000.0 / (high - low), (high + low) / 2
+
+
+def encode(value, slope, middle):
+    return jnp.round(jnp.log2(value) * slope - slope * middle).astype(jnp.int32).astype(jnp.int16)
+
+
+def decode(code, slope, middle):
+    return jnp.exp2(code.astype(jnp.int32).astype(jnp.float32) * (1.0 / slope) + middle)
+
+
+def step_kernel(slope, middle, g_ref, a_ref, u_ref, a_buf, p_buf, q_buf, r_buf, xs, xr, ys, yr, zs, zr, a_sem, x_sem, y_sem, z_sem):
+    count = xs.shape[0]
+    slots, chunk = a_buf.shape[0], a_buf.shape[1]
+    seqs = p_buf.shape[4]
+    half = chunk // 2
+    me = lax.axis_index("col")
+    bx, by, bz = me % 2, (me // 2) % 2, me // 4
+    px = me + 1 - 2 * bx
+    py = me + 2 - 4 * by
+    pz = me + 4 - 8 * bz
+    enc = functools.partial(encode, slope=slope, middle=middle)
+    dec = functools.partial(decode, slope=slope, middle=middle)
+
+    def load(m):
+        slot = lax.rem(m, slots)
+        rows = pl.ds(pl.multiple_of(m * chunk, chunk), chunk)
+        return pltpu.make_async_copy(a_ref.at[rows], a_buf.at[slot], a_sem.at[slot])
+
+    def move(src, dst, sem, m, to):
+        return pltpu.make_async_remote_copy(
+            src_ref=src.at[m], dst_ref=dst.at[m], send_sem=sem.at[0, m], recv_sem=sem.at[1, m],
+            device_id={"col": to}, device_id_type=MESH,
+        )
+
+    for m in range(min(slots, count)):
+        load(m).start()
+    barrier = pltpu.get_barrier_semaphore()
+    for to in (px, py, pz):
+        pl.semaphore_signal(barrier, inc=1, device_id={"col": to}, device_id_type=MESH)
+    pl.semaphore_wait(barrier, 3)
+
+    def body(m, carry):
+        @pl.when(m < count)
+        def _():
+            load(m).wait()
+            slot = lax.rem(m, 2)
+            part = lax.dot_general(
+                g_ref[...], a_buf[lax.rem(m, slots)], (((1,), (1,)), ((), ())), preferred_element_type=jnp.float32
+            )
+            p_buf[slot] = part.reshape(p_buf.shape[1:])
+
+            @pl.when(m + slots < count)
+            def _():
+                load(m + slots).start()
+
+            away = p_buf[slot, :, :, 1 - bx].reshape(4 * seqs, chunk)
+            xs[m] = enc(away)
+            move(xs, xr, x_sem, m, px).start()
+
+        @pl.when((m >= 1) & (m < count + 1))
+        def _():
+            n = m - 1
+            move(xs, xr, x_sem, n, px).wait()
+            got = dec(xr[n]).reshape(2, 2, seqs, chunk)
+            q_buf[...] = p_buf[lax.rem(n, 2), :, :, bx] + got
+            ys[n] = enc(q_buf[:, 1 - by].reshape(2 * seqs, chunk))
+            move(ys, yr, y_sem, n, py).start()
+            r_buf[lax.rem(n, 2)] = q_buf[:, by]
+
+        @pl.when((m >= 2) & (m < count + 2))
+        def _():
+            n = m - 2
+            move(ys, yr, y_sem, n, py).wait()
+            got = dec(yr[n]).reshape(2, seqs, chunk)
+            r_buf[lax.rem(n, 2)] += got
+            away = r_buf[lax.rem(n, 2), 1 - bz]
+            zs[n] = enc(jnp.concatenate([away[:, :half], away[:, half:]], axis=0))
+            move(zs, zr, z_sem, n, pz).start()
+            cols = pl.ds(pl.multiple_of(n * chunk, chunk), chunk)
+            u_ref[:, cols] = r_buf[lax.rem(n, 2), bz]
+
+        @pl.when(m >= 3)
+        def _():
+            n = m - 3
+            move(zs, zr, z_sem, n, pz).wait()
+            got = dec(zr[n])
+            cols = pl.ds(pl.multiple_of(n * chunk, chunk), chunk)
+            u_ref[:, cols] += jnp.concatenate([got[:seqs], got[seqs:]], axis=1)
+
+        return carry
+
+    lax.fori_loop(0, count + 3, body, 0)
+
+
+def step_product(g, transition, lo, hi, seqs, ident):
+    rows, depth = transition.shape
+    chunk = CHUNK
+    count = rows // chunk
+    slope, middle = code_range(lo, hi)
+    i16 = jnp.int16
+    return pl.pallas_call(
+        functools.partial(step_kernel, slope, middle),
+        out_shape=jax.ShapeDtypeStruct((seqs, rows), jnp.float32),
+        in_specs=[pl.BlockSpec(memory_space=pltpu.VMEM), pl.BlockSpec(memory_space=pl.ANY)],
+        out_specs=pl.BlockSpec(memory_space=pltpu.VMEM),
+        scratch_shapes=[
+            pltpu.VMEM((SLOTS, chunk, depth), jnp.bfloat16),
+            pltpu.VMEM((2, 2, 2, 2, seqs, chunk), jnp.float32),
+            pltpu.VMEM((2, 2, seqs, chunk), jnp.float32),
+            pltpu.VMEM((2, 2, seqs, chunk), jnp.float32),
+            pltpu.VMEM((count, 4 * seqs, chunk), i16),
+            pltpu.VMEM((count, 4 * seqs, chunk), i16),
+            pltpu.VMEM((count, 2 * seqs, chunk), i16),
+            pltpu.VMEM((count, 2 * seqs, chunk), i16),
+            pltpu.VMEM((count, 2 * seqs, chunk // 2), i16),
+            pltpu.VMEM((count, 2 * seqs, chunk // 2), i16),
+            pltpu.SemaphoreType.DMA((SLOTS,)),
+            pltpu.SemaphoreType.DMA((2, count)),
+            pltpu.SemaphoreType.DMA((2, count)),
+            pltpu.SemaphoreType.DMA((2, count)),
+        ],
+        cost_estimate=pl.CostEstimate(flops=2 * 8 * seqs * rows * depth, bytes_accessed=2 * rows * depth, transcendentals=0),
+        compiler_params=pltpu.CompilerParams(collective_id=ident, has_side_effects=True, vmem_limit_bytes=56 << 20),
+    )(g, transition)
 
 
 def in_order(arrived, index):
@@ -57,6 +199,21 @@
         got = lax.ppermute(piece, "col", [(c, (c + 2 * k) % col_count) for c in range(col_count)])
         total = total + got.astype(jnp.float32)
     return total
+
+
+def plain_product(weighted_back, transition, scale, scale_mine, col_count, col_index, local_seqs):
+    chunk = transition.shape[0] // CHUNKS
+    pieces = []
+    for k in range(CHUNKS):
+        rows = slice(k * chunk, (k + 1) * chunk)
+        partial = lax.dot_general(
+            weighted_back, transition[rows], (((1,), (1,)), ((), ())), preferred_element_type=jnp.float32
+        )
+        away, keep = split_pair(partial, scale, col_count, col_index, local_seqs)
+        if k < CHUNKS - 1:
+            weighted_back, away = lax.optimization_barrier((weighted_back, away))
+        pieces.append(reduce_scatter(away, keep, col_count, col_index))
+    return jnp.concatenate(pieces, axis=1) / scale_mine
 
 
 def on_device(transition, emission, token_ids, forward, backward_last):
@@ -78,7 +235,6 @@
     beta = backward_last
     scale = jnp.full((seq_total, 1), 64.0, jnp.float32)
     scale_mine = jnp.full((local_seqs, 1), 64.0, jnp.float32)
-    chunk = block_src // CHUNKS
     for step in (1, 0):
         tokens = lax.dynamic_slice_in_dim(token_ids[step], row_index * row_seqs, row_seqs, 0)
         onehot = (tokens[:, None] == columns).astype(jnp.bfloat16)
@@ -88,17 +244,16 @@
         picked[step] = weighted_back[:, :DW]
         if step == 1:
             forward_all = lax.all_gather(forward, "col", axis=1, tiled=True)
-        pieces = []
-        for k in range(CHUNKS):
-            rows = slice(k * chunk, (k + 1) * chunk)
-            partial = lax.dot_general(
-                weighted_back, transition[rows], (((1,), (1,)), ((), ())), preferred_element_type=jnp.float32
-            )
-            away, keep = split_pair(partial, scale, col_count, col_index, local_seqs)
-            if k < CHUNKS - 1:
-                weighted_back, away = lax.optimization_barrier((weighted_back, away))
-            pieces.append(reduce_scatter(away, keep, col_count, col_index))
-        mine = jnp.concatenate(pieces, axis=1) / scale_mine
+        if step == 1:
+            lo = block_dst * A_MIN * E_MIN * B_MIN
+            hi = H * A_MAX * E_MAX * B_MAX
+        else:
+            lo = block_dst * A_MIN * E_MIN * (A_MIN / A_MAX) / (H * F_MAX)
+            hi = H * A_MAX * E_MAX * (A_MAX / A_MIN) / (H * F_MIN)
+        if col_count == 8 and local_seqs % 8 == 0:
+            mine = step_product(weighted_back, transition, lo, hi, local_seqs, step)
+        else:
+            mine = plain_product(weighted_back, transition, scale, scale_mine, col_count, col_index, local_seqs)
         norm = jnp.sum(forward[step].astype(jnp.float32) * mine, axis=1)
         sums = lax.psum(jnp.stack([norm, jnp.sum(mine, axis=1)]), "row")
         sums_all = gather_small(sums, col_count, col_index)

time: 323 us -> 291 us (0.901)
  Pallas kernels: 0 us -> 146 us
  waiting for transfers between devices: 101 us -> 22.6 us
  matrix products: 78.8 us -> 10.5 us
  starting transfers between devices: 99.3 us -> 67.8 us
  local copies, waits for them, and re-layouts: 2.45 us -> 8.33 us
  other arithmetic: 14.3 us -> 8.72 us
    pallas_call x0 -> x2, Pallas kernels: none -> 146 us  [step_product(): pl.pallas_call(functools.partial(step_kernel, slope, middle), out_shape=j...]
    ppermute x16 -> x0, waiting for transfers between devices: 78 us -> none  [the longest x12 39.3 us: reduce_scatter(): lax.ppermute(piece, 'col', [(c, (c + 2 * k) % col_count) for c in range(c...]
    dot_general x4 -> x0, matrix products: 68.2 us -> none  [on_device(): lax.dot_general(weighted_back, transition[rows], (((1,), (1,)), ((), ()))...]
    ppermute x14, starting transfers between devices: 59.1 us -> 25.2 us  [gather_small(): lax.ppermute(value, 'col', [(c, (c + k) % col_count) for c in range(col_c...]
    ppermute x2, starting transfers between devices: 14.1 us -> 41.3 us  [gather_rows(): lax.ppermute(value, 'row', [(r, (r + 2 * k) % row_count) for r in range(r...]
    ppermute x16 -> x0, starting transfers between devices: 23.4 us -> none  [the longest x12 19.2 us: reduce_scatter(): lax.ppermute(piece, 'col', [(c, (c + 2 * k) % col_count) for c in range(c...]
    convert_element_type x8 -> x0, other arithmetic: 7.55 us -> none  [the longest x4 3.96 us: reduce_scatter(): packed = pair.astype(jnp.float16)]
    ppermute x2, waiting for transfers between devices: 0.01 us -> 7.48 us  [on_device(): arrived.append(lax.ppermute(part, ('row', 'col'), moves))]
  transfers between devices with their start and end apart: 37 -> 21, of which waited for: 14 -> 6; matrix products, arithmetic and copies ran while one was open for 26% -> 5% of each run, Pallas kernels for 0% -> 50%
where the time goes in v1:
time: 291 us; the launch traced here: 290 us
  Pallas kernels  146 us (50%)
  starting transfers between devices  67.8 us (23%)
  waiting for transfers between devices  22.6 us (8%)
  between operations  14.5 us (5%)
  blocking collectives  11.7 us (4%)
  matrix products  10.5 us (4%)
  other arithmetic  8.72 us (3%)
  local copies, waits for them, and re-layouts  8.33 us (3%)
    pallas_call x2, Pallas kernels, step_product(): pl.pallas_call(functools.partial(step_kernel, slope, middle), out_shape=j...  146 us
    ppermute x2, starting transfers between devices, gather_rows(): lax.ppermute(value, 'row', [(r, (r + 2 * k) % row_count) for r in range(r...  41.3 us
    ppermute x14, starting transfers between devices, gather_small(): lax.ppermute(value, 'col', [(c, (c + k) % col_count) for c in range(col_c...  25.2 us
    psum x2, blocking collectives, on_device(): sums = lax.psum(jnp.stack([norm, jnp.sum(mine, axis=1)]), 'row')  11.7 us
    ppermute x2, waiting for transfers between devices, gather_rows(): lax.ppermute(value, 'row', [(r, (r + 2 * k) % row_count) for r in range(r...  9.12 us
    dot_general x2, matrix products, on_device(): lax.dot_general(scaled, picked[step], (((0,), (0,)), ((), ())), preferred...  8.77 us
    ppermute x2, waiting for transfers between devices, on_device(): arrived.append(lax.ppermute(part, ('row', 'col'), moves))  7.48 us
  transfers between devices with their start and end apart: 21, of which 6 were waited for; matrix products, arithmetic and copies ran while one was open for 5% of the time, Pallas kernels for 50%

profile of v1, /device:TPU:0, one launch (start us, length us, event | category | flops | bytes accessed | tf_op | source)
XLA Modules:
  0.0 290.4 jit_solution(2151003330670509887)
XLA Ops:
  7.2 0.0 all-gather.2.cloned.1.call-start
  7.2 0.8 fusion.30
  8.0 0.1 fusion.29
  8.1 0.3 copy-done
  8.3 1.4 fusion.4
  9.8 3.0 %collective-permute-start = (bf16[48,4096]{1,0:T(8,128)(2,1)S(1)}, bf16[48,4096]{1,0:T(8,128)(2,1)S(1)}, u32[]{:S(2)}, u32[]{:S(2)}) collective-permute-start(bf16[48,4096]{1,0:T(8,128)(2,1)S(1)} %fusion.4), channel_id=1, source_target_pairs={{0,16},{8,24},{16,0},{24,8},{1,17},{9,25},{17,1},{25,9},{2,18},{10... | collective-permute-start | bytes 1179656 | tf_op jit(solution)/shard_map/ppermute | solution.py:175
  12.8 9.1 %collective-permute-done = bf16[48,4096]{1,0:T(8,128)(2,1)S(1)} collective-permute-done((bf16[48,4096]{1,0:T(8,128)(2,1)S(1)}, bf16[48,4096]{1,0:T(8,128)(2,1)S(1)}, u32[]{:S(2)}, u32[]{:S(2)}) %collective-permute-start) | collective-permute-done | bytes 393248 | tf_op jit(solution)/shard_map/ppermute | solution.py:175
  21.9 0.5 fusion.17
  22.5 0.1 collective-permute-start.1
  22.6 2.2 collective-permute-done.1
  24.8 0.6 select_bitcast_fusion.3
  25.4 0.1 pad_maximum_fusion
  25.6 1.2 copy.7
  26.9 89.7 %shard_map.68 = f32[24,8192]{1,0:T(8,128)} custom-call(bf16[192,4096]{1,0:T(8,128)(2,1)} %bitcast.62, bf16[8192,4096]{1,0:T(8,128)(2,1)} %a_ref.3), custom_call_target="tpu_custom_call" | custom-call | flops 12884901888 | bytes 67108864 | tf_op jit(solution)/shard_map/pallas_call | solution.py:128
  116.6 1.4 fusion.19
  118.0 6.1 %psum.14 = f32[2,24]{1,0:T(2,128)S(1)} all-reduce(f32[2,24]{1,0:T(2,128)S(1)} %pad_maximum_fusion.3), channel_id=1, replica_groups=mesh['row'=4,'col'=8] {'row'}, use_global_device_ids=true, to_apply=%region_2.3 | all-reduce | flops 48 | bytes 384 | tf_op jit(solution)/shard_map/psum | solution.py:258
  124.1 0.1 broadcast_divide_fusion
  124.2 1.5 reshape.51
  125.8 2.2 constant_dynamic-slice_fusion
  128.0 0.2 copy.13
  128.2 0.2 copy.14
  128.5 0.7 collective-permute-start.2
  129.2 0.4 collective-permute-start.3
  129.6 0.1 fusion.28
  129.6 7.5 %collective-permute-done.3 = f32[24,4096]{1,0:T(8,128)} collective-permute-done((f32[24,4096]{1,0:T(8,128)S(1)}, f32[24,4096]{1,0:T(8,128)}, u32[]{:S(2)}, u32[]{:S(2)}) %collective-permute-start.3) | collective-permute-done | bytes 393248 | tf_op jit(solution)/shard_map/ppermute | solution.py:271
  137.1 1.3 fusion.14
  138.4 0.3 fusion.20
  138.7 38.3 %collective-permute-start.4 = (bf16[48,4096]{1,0:T(8,128)(2,1)S(1)}, bf16[48,4096]{1,0:T(8,128)(2,1)S(1)}, u32[]{:S(2)}, u32[]{:S(2)}) collective-permute-start(bf16[48,4096]{1,0:T(8,128)(2,1)S(1)} %fusion.20), channel_id=1, source_target_pairs={{0,16},{8,24},{16,0},{24,8},{1,17},{9,25},{17,1},{25,9},{2,18},{10... | collective-permute-start | bytes 1179656 | tf_op jit(solution)/shard_map/ppermute | solution.py:175
  177.0 1.8 collective-permute-start.12
  178.8 0.5 collective-permute-start.11
  179.4 3.5 %collective-permute-start.9 = (f32[2,24]{1,0:T(2,128)S(1)}, f32[2,24]{1,0:T(2,128)S(1)}, u32[]{:S(2)}, u32[]{:S(2)}) collective-permute-start(f32[2,24]{1,0:T(2,128)S(1)} %psum.14), channel_id=1, source_target_pairs={{0,4},{1,5},{2,6},{3,7},{4,0},{5,1},{6,2},{7,3},{8,12},{9,13},{10,... | collective-permute-start | bytes 584 | tf_op jit(solution)/shard_map/ppermute | solution.py:163
  182.9 0.5 fusion.11
  183.4 0.1 collective-permute-start.5
  183.5 0.1 fusion.33
  183.6 0.6 collective-permute-done.11
  184.2 3.5 %collective-permute-start.8 = (f32[2,24]{1,0:T(2,128)S(1)}, f32[2,24]{1,0:T(2,128)S(1)}, u32[]{:S(2)}, u32[]{:S(2)}) collective-permute-start(f32[2,24]{1,0:T(2,128)S(1)} %psum.14), channel_id=1, source_target_pairs={{0,5},{1,6},{2,7},{3,0},{4,1},{5,2},{6,3},{7,4},{8,13},{9,14},{10,... | collective-permute-start | bytes 584 | tf_op jit(solution)/shard_map/ppermute | solution.py:163
  187.8 1.6 collective-permute-start.7
  189.4 1.9 collective-permute-start.6
  191.3 0.0 collective-permute-done.7
  191.3 1.6 collective-permute-done.6
  193.0 0.6 select_bitcast_fusion.1
  193.6 0.1 pad_maximum_fusion.1
  193.8 1.2 copy.8
  195.0 56.4 %shard_map.69 = f32[24,8192]{1,0:T(8,128)} custom-call(bf16[192,4096]{1,0:T(8,128)(2,1)} %bitcast.64, bf16[8192,4096]{1,0:T(8,128)(2,1)} %a_ref.3), custom_call_target="tpu_custom_call" | custom-call | flops 12884901888 | bytes 67108864 | tf_op jit(solution)/shard_map/pallas_call | solution.py:128
  251.5 1.4 fusion.18
  252.9 5.7 %psum.15 = f32[2,24]{1,0:T(2,128)S(1)} all-reduce(f32[2,24]{1,0:T(2,128)S(1)} %pad_maximum_fusion.4), channel_id=1, replica_groups=mesh['row'=4,'col'=8] {'row'}, use_global_device_ids=true, to_apply=%region_5.6 | all-reduce | flops 48 | bytes 384 | tf_op jit(solution)/shard_map/psum | solution.py:258
  258.6 0.3 collective-permute-start.19
  258.9 2.4 collective-permute-start.18
  261.3 1.9 collective-permute-start.17
  263.2 2.0 collective-permute-start.16
  265.2 0.1 divide_bitcast_fusion
  265.4 1.2 pad_maximum_fusion.2
  266.6 0.8 collective-permute-start.15
  267.4 2.9 %collective-permute-start.14 = (f32[2,24]{1,0:T(2,128)S(1)}, f32[2,24]{1,0:T(2,128)S(1)}, u32[]{:S(2)}, u32[]{:S(2)}) collective-permute-start(f32[2,24]{1,0:T(2,128)S(1)} %psum.15), channel_id=1, source_target_pairs={{0,6},{1,7},{2,0},{3,1},{4,2},{5,3},{6,4},{7,5},{8,14},{9,15},{10,... | collective-permute-start | bytes 584 | tf_op jit(solution)/shard_map/ppermute | solution.py:163
  270.3 0.1 select_select_fusion
  270.5 0.1 fusion.26
  270.6 0.1 div.58
  270.7 2.0 collective-permute-start.13
  272.7 1.6 collective-permute-done.13
  274.3 0.1 fusion.27
  274.4 0.1 div.61
  274.5 3.5 %fusion.7 = f32[8192,128]{1,0:T(8,128)S(1)} fusion(bf16[2,192,8192]{2,1,0:T(8,128)(2,1)} %all-gather.2.cloned.1.call-done, f32[192]{0:T(256)S(1)} %div.58, bf16[192,4096]{1,0:T(8,128)(2,1)} %bitcast.63), kind=kOutput, calls=%fused_computation.12 | convolution fusion | flops 407371776 | bytes 7389952 | tf_op jit(solution)/shard_map/dot_general | solution.py:278
  278.1 0.2 copy-done.10
  278.3 5.2 %fusion.1 = f32[8192,128]{1,0:T(8,128)} fusion(f32[8192,128]{1,0:T(8,128)S(1)} %fusion.7, bf16[2,192,8192]{2,1,0:T(8,128)(2,1)S(1)} %copy-done.10, f32[192]{0:T(256)S(1)} %div.61, bf16[8192,4096]{1,0:T(8,128)(2,1)} %a_ref.3, bf16[192,4096]{1,0:T(8,128)(2,1)} %bitcast.65), kind=kOutput, calls=%fused_computation.2 | convolution fusion | flops 411566080 | bytes 13681664 | tf_op jit(solution)/shard_map/dot_general | solution.py:278
  (62 shorter events, 0.2 us)
Async XLA Ops:
  7.2 1.2 copy-start
  7.2 267.3 %all-gather.2.cloned.1.call-start = ((), (), s32[]{:S(2)}) async-start(), calls=%async_computation | async-start | bytes 7077888 | tf_op jit(solution)/shard_map/all_gather | solution.py:246
  9.8 12.1 %collective-permute-start = (bf16[48,4096]{1,0:T(8,128)(2,1)S(1)}, bf16[48,4096]{1,0:T(8,128)(2,1)S(1)}, u32[]{:S(2)}, u32[]{:S(2)}) collective-permute-start(bf16[48,4096]{1,0:T(8,128)(2,1)S(1)} %fusion.4), channel_id=1, source_target_pairs={{0,16},{8,24},{16,0},{24,8},{1,17},{9,25},{17,1},{25,9},{2,18},{10... | collective-permute-start | bytes 1179656 | tf_op jit(solution)/shard_map/ppermute | solution.py:175
  22.5 2.4 collective-permute-start.1
  26.8 89.7 %copy-start.3 = (bf16[2,24,8192]{2,1,0:T(8,128)(2,1)S(1)}, bf16[2,24,8192]{2,1,0:T(8,128)(2,1)}, u32[]{:S(2)}) copy-start(bf16[2,24,8192]{2,1,0:T(8,128)(2,1)} %param.8) | copy-start | bytes 2359300
  116.6 7.5 %copy-start.1 = (f32[24,8192]{1,0:T(8,128)S(1)}, f32[24,8192]{1,0:T(8,128)}, u32[]{:S(2)}) copy-start(f32[24,8192]{1,0:T(8,128)} %shard_map.68) | copy-start | bytes 2359300
  128.5 1.2 collective-permute-start.2
  129.2 7.9 %collective-permute-start.3 = (f32[24,4096]{1,0:T(8,128)S(1)}, f32[24,4096]{1,0:T(8,128)}, u32[]{:S(2)}, u32[]{:S(2)}) collective-permute-start(f32[24,4096]{1,0:T(8,128)S(1)} %bitcast.74), channel_id=1, source_target_pairs={{0,1},{1,0},{2,9},{3,8},{4,17},{5,16},{6,25},{7,24},{8,3},{9,2},{1... | collective-permute-start | bytes 1179656 | tf_op jit(solution)/shard_map/ppermute | solution.py:271
  138.7 44.2 %collective-permute-start.4 = (bf16[48,4096]{1,0:T(8,128)(2,1)S(1)}, bf16[48,4096]{1,0:T(8,128)(2,1)S(1)}, u32[]{:S(2)}, u32[]{:S(2)}) collective-permute-start(bf16[48,4096]{1,0:T(8,128)(2,1)S(1)} %fusion.20), channel_id=1, source_target_pairs={{0,16},{8,24},{16,0},{24,8},{1,17},{9,25},{17,1},{25,9},{2,18},{10... | collective-permute-start | bytes 1179656 | tf_op jit(solution)/shard_map/ppermute | solution.py:175
  177.0 89.6 %collective-permute-start.12 = (f32[2,24]{1,0:T(2,128)S(1)}, f32[2,24]{1,0:T(2,128)S(1)}, u32[]{:S(2)}, u32[]{:S(2)}) collective-permute-start(f32[2,24]{1,0:T(2,128)S(1)} %psum.14), channel_id=1, source_target_pairs={{0,1},{1,2},{2,3},{3,4},{4,5},{5,6},{6,7},{7,0},{8,9},{9,10},{10,1... | collective-permute-start | bytes 584 | tf_op jit(solution)/shard_map/ppermute | solution.py:163
  178.8 5.4 %collective-permute-start.11 = (f32[2,24]{1,0:T(2,128)S(1)}, f32[2,24]{1,0:T(2,128)S(1)}, u32[]{:S(2)}, u32[]{:S(2)}) collective-permute-start(f32[2,24]{1,0:T(2,128)S(1)} %psum.14), channel_id=1, source_target_pairs={{0,2},{1,3},{2,4},{3,5},{4,6},{5,7},{6,0},{7,1},{8,10},{9,11},{10,... | collective-permute-start | bytes 584 | tf_op jit(solution)/shard_map/ppermute | solution.py:163
  179.4 8.4 %collective-permute-start.10 = (f32[2,24]{1,0:T(2,128)S(1)}, f32[2,24]{1,0:T(2,128)S(1)}, u32[]{:S(2)}, u32[]{:S(2)}) collective-permute-start(f32[2,24]{1,0:T(2,128)S(1)} %psum.14), channel_id=1, source_target_pairs={{0,3},{1,4},{2,5},{3,6},{4,7},{5,0},{6,1},{7,2},{8,11},{9,12},{10,... | collective-permute-start | bytes 584 | tf_op jit(solution)/shard_map/ppermute | solution.py:163
  179.4 10.0 %collective-permute-start.9 = (f32[2,24]{1,0:T(2,128)S(1)}, f32[2,24]{1,0:T(2,128)S(1)}, u32[]{:S(2)}, u32[]{:S(2)}) collective-permute-start(f32[2,24]{1,0:T(2,128)S(1)} %psum.14), channel_id=1, source_target_pairs={{0,4},{1,5},{2,6},{3,7},{4,0},{5,1},{6,2},{7,3},{8,12},{9,13},{10,... | collective-permute-start | bytes 584 | tf_op jit(solution)/shard_map/ppermute | solution.py:163
  183.4 9.5 %collective-permute-start.5 = (bf16[2,48,4096]{2,1,0:T(8,128)(2,1)S(1)}, bf16[2,48,4096]{2,1,0:T(8,128)(2,1)S(1)}, u32[]{:S(2)}, u32[]{:S(2)}) collective-permute-start(bf16[2,48,4096]{2,1,0:T(8,128)(2,1)S(1)} %fusion.11), channel_id=1, source_target_pairs={{0,8},{8,0},{16,24},{24,16},{1,9},{9,1},{17,25},{25,17},{2,10},{10... | collective-permute-start | bytes 2359304 | tf_op jit(solution)/shard_map/ppermute | solution.py:177
  184.2 9.4 %copy-start.4 = (f32[2,24]{1,0:T(2,128)}, f32[2,24]{1,0:T(2,128)S(1)}, u32[]{:S(2)}) copy-start(f32[2,24]{1,0:T(2,128)S(1)} %collective-permute-done.11) | copy-start | bytes 580
  184.2 7.1 %collective-permute-start.8 = (f32[2,24]{1,0:T(2,128)S(1)}, f32[2,24]{1,0:T(2,128)S(1)}, u32[]{:S(2)}, u32[]{:S(2)}) collective-permute-start(f32[2,24]{1,0:T(2,128)S(1)} %psum.14), channel_id=1, source_target_pairs={{0,5},{1,6},{2,7},{3,0},{4,1},{5,2},{6,3},{7,4},{8,13},{9,14},{10,... | collective-permute-start | bytes 584 | tf_op jit(solution)/shard_map/ppermute | solution.py:163
  187.8 5.8 %copy-start.5 = (f32[2,24]{1,0:T(2,128)}, f32[2,24]{1,0:T(2,128)S(1)}, u32[]{:S(2)}) copy-start(f32[2,24]{1,0:T(2,128)S(1)} %collective-permute-done.10) | copy-start | bytes 580
  187.8 3.6 %collective-permute-start.7 = (f32[2,24]{1,0:T(2,128)S(1)}, f32[2,24]{1,0:T(2,128)S(1)}, u32[]{:S(2)}, u32[]{:S(2)}) collective-permute-start(f32[2,24]{1,0:T(2,128)S(1)} %psum.14), channel_id=1, source_target_pairs={{0,6},{1,7},{2,0},{3,1},{4,2},{5,3},{6,4},{7,5},{8,14},{9,15},{10,... | collective-permute-start | bytes 584 | tf_op jit(solution)/shard_map/ppermute | solution.py:163
  189.4 4.2 %copy-start.6 = (f32[2,24]{1,0:T(2,128)}, f32[2,24]{1,0:T(2,128)S(1)}, u32[]{:S(2)}) copy-start(f32[2,24]{1,0:T(2,128)S(1)} %collective-permute-done.9) | copy-start | bytes 580
  189.4 3.6 %collective-permute-start.6 = (f32[2,24]{1,0:T(2,128)S(1)}, f32[2,24]{1,0:T(2,128)S(1)}, u32[]{:S(2)}, u32[]{:S(2)}) collective-permute-start(f32[2,24]{1,0:T(2,128)S(1)} %psum.14), channel_id=1, source_target_pairs={{0,7},{1,0},{2,1},{3,2},{4,3},{5,4},{6,5},{7,6},{8,15},{9,8},{10,9... | collective-permute-start | bytes 584 | tf_op jit(solution)/shard_map/ppermute | solution.py:163
  191.3 2.3 copy-start.7
  191.3 2.3 copy-start.8
  192.9 0.7 copy-start.9
  251.4 13.7 %copy-start.2 = (f32[24,8192]{1,0:T(8,128)S(1)}, f32[24,8192]{1,0:T(8,128)}, u32[]{:S(2)}) copy-start(f32[24,8192]{1,0:T(8,128)} %shard_map.69) | copy-start | bytes 2359300
  258.6 8.8 %collective-permute-start.19 = (f32[2,24]{1,0:T(2,128)S(1)}, f32[2,24]{1,0:T(2,128)S(1)}, u32[]{:S(2)}, u32[]{:S(2)}) collective-permute-start(f32[2,24]{1,0:T(2,128)S(1)} %psum.15), channel_id=1, source_target_pairs={{0,1},{1,2},{2,3},{3,4},{4,5},{5,6},{6,7},{7,0},{8,9},{9,10},{10,1... | collective-permute-start | bytes 584 | tf_op jit(solution)/shard_map/ppermute | solution.py:163
  258.9 11.8 %collective-permute-start.18 = (f32[2,24]{1,0:T(2,128)S(1)}, f32[2,24]{1,0:T(2,128)S(1)}, u32[]{:S(2)}, u32[]{:S(2)}) collective-permute-start(f32[2,24]{1,0:T(2,128)S(1)} %psum.15), channel_id=1, source_target_pairs={{0,2},{1,3},{2,4},{3,5},{4,6},{5,7},{6,0},{7,1},{8,10},{9,11},{10,... | collective-permute-start | bytes 584 | tf_op jit(solution)/shard_map/ppermute | solution.py:163
  261.3 11.4 %collective-permute-start.17 = (f32[2,24]{1,0:T(2,128)S(1)}, f32[2,24]{1,0:T(2,128)S(1)}, u32[]{:S(2)}, u32[]{:S(2)}) collective-permute-start(f32[2,24]{1,0:T(2,128)S(1)} %psum.15), channel_id=1, source_target_pairs={{0,3},{1,4},{2,5},{3,6},{4,7},{5,0},{6,1},{7,2},{8,11},{9,12},{10,... | collective-permute-start | bytes 584 | tf_op jit(solution)/shard_map/ppermute | solution.py:163
  263.2 9.5 %collective-permute-start.16 = (f32[2,24]{1,0:T(2,128)S(1)}, f32[2,24]{1,0:T(2,128)S(1)}, u32[]{:S(2)}, u32[]{:S(2)}) collective-permute-start(f32[2,24]{1,0:T(2,128)S(1)} %psum.15), channel_id=1, source_target_pairs={{0,4},{1,5},{2,6},{3,7},{4,0},{5,1},{6,2},{7,3},{8,12},{9,13},{10,... | collective-permute-start | bytes 584 | tf_op jit(solution)/shard_map/ppermute | solution.py:163
  265.3 5.1 %slice-start = ((f32[2,24]{1,0:T(2,128)}), f32[1,24]{1,0:T(1,128)S(1)}, s32[]{:S(2)}) async-start(f32[2,24]{1,0:T(2,128)} %copy-done.4), calls=%async_computation.1 | async-start | bytes 1024 | tf_op jit(solution)/shard_map/slice | solution.py:260
  265.3 5.1 %slice-start.1 = ((f32[2,24]{1,0:T(2,128)}), f32[1,24]{1,0:T(1,128)S(1)}, s32[]{:S(2)}) async-start(f32[2,24]{1,0:T(2,128)} %copy-done.5), calls=%async_computation.2 | async-start | bytes 1024 | tf_op jit(solution)/shard_map/slice | solution.py:260
  265.3 5.1 %slice-start.2 = ((f32[2,24]{1,0:T(2,128)}), f32[1,24]{1,0:T(1,128)S(1)}, s32[]{:S(2)}) async-start(f32[2,24]{1,0:T(2,128)} %copy-done.6), calls=%async_computation.3 | async-start | bytes 1024 | tf_op jit(solution)/shard_map/slice | solution.py:260
  265.3 5.1 %slice-start.3 = ((f32[2,24]{1,0:T(2,128)}), f32[1,24]{1,0:T(1,128)S(1)}, s32[]{:S(2)}) async-start(f32[2,24]{1,0:T(2,128)} %copy-done.7), calls=%async_computation.4 | async-start | bytes 1024 | tf_op jit(solution)/shard_map/slice | solution.py:260
  265.3 5.1 %slice-start.4 = ((f32[2,24]{1,0:T(2,128)}), f32[1,24]{1,0:T(1,128)S(1)}, s32[]{:S(2)}) async-start(f32[2,24]{1,0:T(2,128)} %copy-done.8), calls=%async_computation.5 | async-start | bytes 1024 | tf_op jit(solution)/shard_map/slice | solution.py:260
  265.4 5.1 %slice-start.5 = ((f32[2,24]{1,0:T(2,128)}), f32[1,24]{1,0:T(1,128)S(1)}, s32[]{:S(2)}) async-start(f32[2,24]{1,0:T(2,128)} %copy-done.9), calls=%async_computation.6 | async-start | bytes 1024 | tf_op jit(solution)/shard_map/slice | solution.py:260
  266.6 6.1 %collective-permute-start.15 = (f32[2,24]{1,0:T(2,128)S(1)}, f32[2,24]{1,0:T(2,128)S(1)}, u32[]{:S(2)}, u32[]{:S(2)}) collective-permute-start(f32[2,24]{1,0:T(2,128)S(1)} %psum.15), channel_id=1, source_target_pairs={{0,5},{1,6},{2,7},{3,0},{4,1},{5,2},{6,3},{7,4},{8,13},{9,14},{10,... | collective-permute-start | bytes 584 | tf_op jit(solution)/shard_map/ppermute | solution.py:163
  267.4 5.3 %collective-permute-start.14 = (f32[2,24]{1,0:T(2,128)S(1)}, f32[2,24]{1,0:T(2,128)S(1)}, u32[]{:S(2)}, u32[]{:S(2)}) collective-permute-start(f32[2,24]{1,0:T(2,128)S(1)} %psum.15), channel_id=1, source_target_pairs={{0,6},{1,7},{2,0},{3,1},{4,2},{5,3},{6,4},{7,5},{8,14},{9,15},{10,... | collective-permute-start | bytes 584 | tf_op jit(solution)/shard_map/ppermute | solution.py:163
  270.7 3.6 %collective-permute-start.13 = (f32[2,24]{1,0:T(2,128)S(1)}, f32[2,24]{1,0:T(2,128)S(1)}, u32[]{:S(2)}, u32[]{:S(2)}) collective-permute-start(f32[2,24]{1,0:T(2,128)S(1)} %psum.15), channel_id=1, source_target_pairs={{0,7},{1,0},{2,1},{3,2},{4,3},{5,4},{6,5},{7,6},{8,15},{9,8},{10,9... | collective-permute-start | bytes 584 | tf_op jit(solution)/shard_map/ppermute | solution.py:163
  274.5 3.8 %copy-start.10 = (bf16[2,192,8192]{2,1,0:T(8,128)(2,1)S(1)}, bf16[2,192,8192]{2,1,0:T(8,128)(2,1)}, u32[]{:S(2)}) copy-start(bf16[2,192,8192]{2,1,0:T(8,128)(2,1)} %all-gather.2.cloned.1.call-done) | copy-start | bytes 18874372
Sparse Core Ops, SparseCore 0:
  22.7 137.8 all-gather.1

commit v2 on v0

--- a/solution.py
+++ b/solution.py
@@ -1,12 +1,560 @@
+import functools
+import math
+
 import jax
 import jax.numpy as jnp
 from jax import lax
+from jax.experimental import pallas as pl
+from jax.experimental.pallas import tpu as pltpu
 from jax.sharding import PartitionSpec as P
 
 H = 32768
 N = 192
 DW = 128
 CHUNKS = 2
+A_MIN, A_MAX = 1.5258789e-06, 0.0024414062
+E_MIN, E_MAX = 0.0099487305, 1.0
+B_MIN, B_MAX = 0.1, 10.0
+CHUNK = 512
+SLOTS = 4
+MESH = pl.DeviceIdType.MESH
+
+
+def code_range(lo, hi):
+    low = math.log2(lo) - 0.5
+    high = math.log2(hi) + 0.5
+    return 65000.0 / (high - low), (high + low) / 2
+
+
+def encode(value, slope, middle):
+    return jnp.round(jnp.log2(value) * slope - slope * middle).astype(jnp.int32).astype(jnp.int16)
+
+
+def decode(code, slope, middle):
+    return jnp.exp2(code.astype(jnp.int32).astype(jnp.float32) * (1.0 / slope) + middle)
+
+
+def big_kernel(
+    codes, hot1_ref, hot0_ref, emit_ref, last_ref, fwd_ref, a_ref,
+    u_ref, zall_ref, gw_ref, fall_ref,
+    a_buf, p_buf, q_buf, g1, g0, zacc, zs, zr, zc, us, ug,
+    xs, xr, as_, ar, bs, br, cs, cr,
+    a_sem, x_sem, al_sem, b_sem, c_sem, gy_sem, gc_sem, gd_sem, us_sem, ug_sem, uc_sem, zr_sem, zc_sem, fx_sem, fz_sem,
+):
+    count = xs.shape[1]
+    slots, chunk = a_buf.shape[0], a_buf.shape[1]
+    seqs = q_buf.shape[2]
+    half = chunk // 2
+    per = count // 2
+    deep = q_buf.shape[0]
+    r = lax.axis_index("row")
+    c = lax.axis_index("col")
+    y, k, z, x = r // 2, r % 2, c // 2, c % 2
+    side = z // 2
+    outer = (z == 0) | (z == 3)
+    z_in, z_out = 1 + side, 3 * side
+    z_in2, z_out2 = 2 - side, 3 - 3 * side
+    px = 2 * z + 1 - x
+    r1, r2 = r + 1 - 2 * k, (r + 2) % 4
+    part_cols = g1.shape[2] // 4
+
+    def remote(src, dst, send, recv, row, col):
+        return pltpu.make_async_remote_copy(
+            src_ref=src, dst_ref=dst, send_sem=send, recv_sem=recv,
+            device_id={"row": row, "col": col}, device_id_type=MESH,
+        )
+
+    def load(g):
+        slot = lax.rem(g, slots)
+        n = lax.rem(g, count)
+        at = pl.ds(pl.multiple_of(((n % 2) * per + n // 2) * chunk, chunk), chunk)
+        return pltpu.make_async_copy(a_ref.at[at], a_buf.at[slot], a_sem.at[slot])
+
+    for g in range(slots):
+        load(g).start()
+    barrier = pltpu.get_barrier_semaphore()
+    me = r * 8 + c
+
+    def greet(i, carry):
+        @pl.when(i != me)
+        def _():
+            pl.semaphore_signal(barrier, inc=1, device_id={"row": i // 8, "col": i % 8}, device_id_type=MESH)
+        return carry
+
+    lax.fori_loop(0, 32, greet, 0)
+
+    for j in range(4):
+        cols = slice(j * part_cols, (j + 1) * part_cols)
+        emitted = jnp.dot(hot1_ref[...], emit_ref[:, cols], preferred_element_type=jnp.float32)
+        g1[r, :, cols] = (emitted * last_ref[:, cols]).astype(jnp.bfloat16)
+    wide = fall_ref.shape[3]
+    for time in range(2):
+        for j in range(4):
+            left = slice(j * wide // 4, (j + 1) * wide // 4)
+            right = slice(wide + j * wide // 4, wide + (j + 1) * wide // 4)
+            pair = [fwd_ref[time, :, left].astype(jnp.float32), fwd_ref[time, :, right].astype(jnp.float32)]
+            fall_ref[time, c, :, left] = jnp.concatenate(pair, axis=0).astype(jnp.bfloat16)
+    pl.semaphore_wait(barrier, 31)
+
+    def g_move(block, j, sem, to):
+        at = g1.at[block, :, pl.ds(j * part_cols, part_cols)]
+        return remote(at, at, sem.at[0, j], sem.at[1, j], to, c)
+
+    for j in range(4):
+        g_move(r, j, gy_sem, r2).start()
+        g_move(r, j, gc_sem, r1).start()
+
+    def fx_move(i, t, block):
+        at = fall_ref.at[t, block]
+        return remote(at, at, fx_sem.at[0, i], fx_sem.at[1, i], r, px)
+
+    def fz_move(way, kind, src, to):
+        t = 0 if kind == 0 else 1
+        block = 2 * src + (x if kind < 2 else 1 - x)
+        at = fall_ref.at[t, block]
+        return remote(at, at, fz_sem.at[0, way, kind, src], fz_sem.at[1, way, kind, src], r, 2 * to + x)
+
+    def fz_send(kind, d):
+        @pl.when((z < 3) & (z - d + 1 >= 0))
+        def _():
+            fz_move(0, kind, z - d + 1, z + 1).start()
+
+        @pl.when((z > 0) & (z + d - 1 <= 3))
+        def _():
+            fz_move(1, kind, z + d - 1, z - 1).start()
+
+    def fz_sent(kind, d):
+        @pl.when((z < 3) & (z - d + 1 >= 0))
+        def _():
+            fz_move(0, kind, z - d + 1, z + 1).wait_send()
+
+        @pl.when((z > 0) & (z + d - 1 <= 3))
+        def _():
+            fz_move(1, kind, z + d - 1, z - 1).wait_send()
+
+    def fz_got(kind, d):
+        @pl.when(z - d >= 0)
+        def _():
+            fz_move(0, kind, z - d, z).wait_recv()
+
+        @pl.when(z + d <= 3)
+        def _():
+            fz_move(1, kind, z + d, z).wait_recv()
+
+    def fx_each(d, act):
+        @pl.when(z - d >= 0)
+        def _():
+            act(fx_move(1 + z - d, 0, 2 * (z - d) + x))
+
+        if d:
+            @pl.when(z + d <= 3)
+            def _():
+                act(fx_move(1 + z + d, 0, 2 * (z + d) + x))
+
+    def start(move):
+        move.start()
+
+    fx_move(0, 1, c).start()
+    fz_send(0, 1)
+    for j in range(4):
+        g_move(r, j, gy_sem, r2).wait_recv()
+        g_move(r2, j, gd_sem, r1).start()
+    for j in range(4):
+        g_move(r, j, gc_sem, r1).wait()
+        g_move(r2, j, gd_sem, r1).wait()
+        g_move(r, j, gy_sem, r2).wait_send()
+    fx_each(0, start)
+    fx_move(0, 1, c).wait_recv()
+    fz_send(1, 1)
+    fz_send(2, 1)
+
+    def tick1a():
+        fz_got(0, 1)
+        fz_send(0, 2)
+
+    def tick1b():
+        for kind in (1, 2):
+            fz_got(kind, 1)
+            fz_send(kind, 2)
+
+    def tick1c():
+        fz_got(0, 2)
+        fz_send(0, 3)
+        fx_each(1, start)
+
+    def tick1d():
+        fx_each(2, start)
+
+    def tick0a():
+        for kind in (1, 2):
+            fz_got(kind, 2)
+            fz_send(kind, 3)
+
+    def tick0b():
+        fz_got(0, 3)
+        fx_each(3, start)
+
+    def two(value):
+        return jnp.concatenate([value[:, :half], value[:, half:]], axis=0)
+
+    def one(value):
+        n = value.shape[0] // 2
+        return jnp.concatenate([value[:n], value[n:]], axis=1)
+
+    zacc[...] = jnp.zeros(zacc.shape, jnp.float32)
+
+    def run(ti, g_buf, ticks):
+        time = 1 - ti
+        slope, middle = codes[ti]
+        enc = functools.partial(encode, slope=slope, middle=middle)
+        dec = functools.partial(decode, slope=slope, middle=middle)
+
+        def x_move(n):
+            return remote(xs.at[ti, n], xr.at[ti, n], x_sem.at[0, ti, n], x_sem.at[1, ti, n], r, px)
+
+        def a_move(n):
+            return remote(as_.at[ti, n], ar.at[ti, n], al_sem.at[0, ti, n], al_sem.at[1, ti, n], r, 2 * z_in + x)
+
+        def b_move(n):
+            return remote(bs.at[ti, n], br.at[ti, n], b_sem.at[0, ti, n], b_sem.at[1, ti, n], r, 2 * z_in2 + x)
+
+        def c_move(n):
+            return remote(cs.at[ti, n], cr.at[ti, n], c_sem.at[0, ti, n], c_sem.at[1, ti, n], r, 2 * z_out + x)
+
+        def u_move(n, yy, to_col, q):
+            return remote(us.at[n], ug.at[q, c], us_sem.at[yy, n], ug_sem.at[q, c], 2 * yy + k, to_col)
+
+        def uc_move(q):
+            return remote(ug.at[q], ug.at[q], uc_sem.at[0, q], uc_sem.at[1, q], r1, c)
+
+        def body(m, carry):
+            @pl.when(m < count)
+            def _():
+                g = m + ti * count
+                load(g).wait()
+                part = lax.dot_general(
+                    g_buf[...].reshape(8 * seqs, g_buf.shape[-1]), a_buf[lax.rem(g, slots)], (((1,), (1,)), ((), ())),
+                    preferred_element_type=jnp.float32,
+                )
+                p_buf[...] = part.reshape(p_buf.shape)
+
+                @pl.when(g + slots < 2 * count)
+                def _():
+                    load(g + slots).start()
+
+                xs[ti, m] = enc(p_buf[:, 1 - x].reshape(4 * seqs, chunk))
+                x_move(m).start()
+                q_buf[lax.rem(m, deep)] = p_buf[:, x]
+
+            for at, act in ticks:
+                pl.when(m == at)(act)
+
+            @pl.when((m >= LAG) & (m < count + LAG))
+            def _():
+                n = m - LAG
+                s = lax.rem(n, deep)
+                x_move(n).wait()
+                q_buf[s] += dec(xr[ti, n]).reshape(4, seqs, chunk)
+
+                @pl.when(outer)
+                def _():
+                    three = jnp.concatenate([q_buf[s, z_in], q_buf[s, z_in2], q_buf[s, z_out2]], axis=0)
+                    as_[ti, n] = enc(two(three))
+                    a_move(n).start()
+
+            @pl.when((m >= 2 * LAG) & (m < count + 2 * LAG) & jnp.logical_not(outer))
+            def _():
+                n = m - 2 * LAG
+                s = lax.rem(n, deep)
+                a_move(n).wait_recv()
+                got = one(dec(ar[ti, n]))
+                q_buf[s, z_in] += got[:seqs]
+                pair = jnp.concatenate([q_buf[s, z_in2] + got[seqs:2 * seqs], q_buf[s, z_out2] + got[2 * seqs:]], axis=0)
+                bs[ti, n] = enc(pair)
+                b_move(n).start()
+
+            @pl.when((m >= 3 * LAG) & (m < count + 3 * LAG) & jnp.logical_not(outer))
+            def _():
+                n = m - 3 * LAG
+                s = lax.rem(n, deep)
+                b_move(n).wait()
+                got = dec(br[ti, n])
+                q_buf[s, z_in] += got[:seqs]
+                cs[ti, n] = enc(two(q_buf[s, z_out] + got[seqs:]))
+                c_move(n).start()
+
+            @pl.when((m >= 4 * LAG) & (m < count + 4 * LAG))
+            def _():
+                n = m - 4 * LAG
+                s = lax.rem(n, deep)
+
+                @pl.when(outer)
+                def _():
+                    c_move(n).wait_recv()
+                    a_move(n).wait_send()
+                    q_buf[s, z_out] += one(dec(cr[ti, n]))
+
+                @pl.when(jnp.logical_not(outer))
+                def _():
+                    c_move(n).wait_send()
+
+                value = q_buf[s, z]
+                cols = pl.ds(pl.multiple_of(((n % 2) * per + n // 2) * chunk, chunk), chunk)
+                u_ref[time, :, cols] = value
+                weighed = fwd_ref[time, :, cols].astype(jnp.float32) * value
+                total = zacc[time]
+                for i in range(chunk // 128):
+                    total = total + weighed[:, i * 128:(i + 1) * 128]
+                zacc[time] = total
+                if ti == 0:
+                    h = n % 2
+                    q = n // 2
+                    to_col = 2 * r + h
+                    us[n] = enc(two(value))
+                    for yy in range(2):
+                        mine = (yy == y) & (to_col == c)
+
+                        @pl.when(mine)
+                        def _():
+                            ug[q, c] = us[n]
+
+                        @pl.when(jnp.logical_not(mine))
+                        def _():
+                            u_move(n, yy, to_col, q).start()
+
+            if ti == 0:
+                ahead = m - (4 * LAG + GAP + x)
+                direct = k == z % 2
+
+                @pl.when((ahead >= 0) & (ahead < 2 * per) & (ahead % 2 == 0) & direct)
+                def _():
+                    q = ahead // 2
+                    for src in range(8):
+                        @pl.when(jnp.logical_not((r == z) & (c == src)))
+                        def _():
+                            remote(us.at[0], ug.at[q, src], us_sem.at[0, 0], ug_sem.at[q, src], r, src).wait_recv()
+                    uc_move(q).start()
+
+                later = ahead - GAP2
+
+                @pl.when((later >= 0) & (later < 2 * per) & (later % 2 == 0))
+                def _():
+                    q = later // 2
+
+                    @pl.when(direct)
+                    def _():
+                        uc_move(q).wait_send()
+
+                    @pl.when(jnp.logical_not(direct))
+                    def _():
+                        uc_move(q).wait_recv()
+
+                    cols = pl.ds(pl.multiple_of(q * chunk, chunk), chunk)
+                    emitted = jnp.dot(hot0_ref[...], emit_ref[:, cols], preferred_element_type=jnp.float32)
+                    for src in range(8):
+                        value = one(dec(ug[q, src])) * emitted[src * seqs:(src + 1) * seqs]
+                        p_buf[src // 2, src % 2] = value
+                    g0[:, cols] = p_buf[...].reshape(8 * seqs, chunk).astype(jnp.bfloat16)
+
+            return carry
+
+        steps = count + 4 * LAG
+        if ti == 0:
+            steps += GAP + GAP2
+        lax.fori_loop(0, steps, body, 0)
+        if ti == 0:
+            def sent(n, carry):
+                h = n % 2
+                for yy in range(2):
+                    mine = (yy == y) & (2 * r + h == c)
+
+                    @pl.when(jnp.logical_not(mine))
+                    def _():
+                        u_move(n, yy, 2 * r + h, n // 2).wait_send()
+                return carry
+
+            lax.fori_loop(0, count, sent, 0)
+
+    def z_move(time, d):
+        return remote(zs.at[time], zr.at[time, d], zr_sem.at[0, time, d], zr_sem.at[1, time, d], lax.rem(r + d, 4), c)
+
+    def z_start(time):
+        zs[time] = jnp.broadcast_to(jnp.sum(zacc[time], axis=1, keepdims=True), zs.shape[1:])
+        for d in range(1, 4):
+            z_move(time, d).start()
+
+    run(0, g1, TICKS1(tick1a, tick1b, tick1c, tick1d))
+    z_start(1)
+    run(1, g0, TICKS0(tick0a, tick0b))
+    z_start(0)
+    gw_ref[1] = g1[:, :, :128].reshape(8 * seqs, 128)
+    gw_ref[0] = g0[:, :128]
+    for time in (1, 0):
+        for d in range(1, 4):
+            z_move(time, d).wait()
+        zr[time, 0] = zs[time]
+
+        def arrived(i):
+            return zr[time, lax.rem(r + 4 - i, 4)]
+
+        zc[time] = (arrived(0) + arrived(1)) + (arrived(2) + arrived(3))
+
+    def zc_move(d):
+        return remote(zc, zall_ref.at[c], zc_sem.at[0, d], zc_sem.at[1, d], r, lax.rem(c + d, 8))
+
+    for d in range(1, 8):
+        zc_move(d).start()
+    zall_ref[c] = zc[...]
+    fx_move(0, 1, c).wait_send()
+    for d in range(4):
+        fx_each(d, lambda move: move.wait_send())
+    for src in range(4):
+        fx_move(1 + src, 0, 2 * src + x).wait_recv()
+    for kind in range(3):
+        for d in (1, 2, 3):
+            fz_sent(kind, d)
+    for kind in (1, 2):
+        fz_got(kind, 3)
+    for d in range(1, 8):
+        zc_move(d).wait()
+
+
+LAG = 2
+GAP = 3
+GAP2 = 2
+
+
+def TICKS1(a, b, c, d):
+    return ((3, a), (10, b), (16, c), (21, d))
+
+
+def TICKS0(a, b):
+    return ((1, a), (6, b))
+
+
+def big_call(hot1, hot0, emission, last, forward, transition):
+    rows, depth = transition.shape
+    seqs = forward.shape[1]
+    chunk = CHUNK
+    count = rows // chunk
+    total = 8 * seqs
+    i16, f32, bf16 = jnp.int16, jnp.float32, jnp.bfloat16
+    lo1, hi1 = depth * A_MIN * E_MIN * B_MIN, H * A_MAX * E_MAX * B_MAX
+    lo0, hi0 = depth * A_MIN * E_MIN * (H * A_MIN * E_MIN * B_MIN), H * A_MAX * E_MAX * hi1
+    codes = (code_range(lo1, hi1), code_range(lo0, hi0))
+    dma = pltpu.SemaphoreType.DMA
+    vmem = pl.BlockSpec(memory_space=pltpu.VMEM)
+    anyw = pl.BlockSpec(memory_space=pl.ANY)
+    return pl.pallas_call(
+        functools.partial(big_kernel, codes),
+        out_shape=(
+            jax.ShapeDtypeStruct((2, seqs, rows), f32),
+            jax.ShapeDtypeStruct((8, 2, seqs, 128), f32),
+            jax.ShapeDtypeStruct((2, total, 128), bf16),
+            jax.ShapeDtypeStruct((2, 8, 2 * seqs, rows // 2), bf16),
+        ),
+        in_specs=[vmem] * 5 + [anyw],
+        out_specs=(vmem, vmem, vmem, vmem),
+        scratch_shapes=[
+            pltpu.VMEM((SLOTS, chunk, depth), bf16),
+            pltpu.VMEM((4, 2, seqs, chunk), f32),
+            pltpu.VMEM((4 * LAG + 1, 4, seqs, chunk), f32),
+            pltpu.VMEM((4, 2 * seqs, depth), bf16),
+            pltpu.VMEM((total, depth), bf16),
+            pltpu.VMEM((2, seqs, 128), f32),
+            pltpu.VMEM((2, seqs, 128), f32),
+            pltpu.VMEM((2, 4, seqs, 128), f32),
+            pltpu.VMEM((2, seqs, 128), f32),
+            pltpu.VMEM((count, 2 * seqs, chunk // 2), i16),
+            pltpu.VMEM((count // 2, 8, 2 * seqs, chunk // 2), i16),
+            pltpu.VMEM((2, count, 4 * seqs, chunk), i16),
+            pltpu.VMEM((2, count, 4 * seqs, chunk), i16),
+            pltpu.VMEM((2, count, 6 * seqs, chunk // 2), i16),
+            pltpu.VMEM((2, count, 6 * seqs, chunk // 2), i16),
+            pltpu.VMEM((2, count, 2 * seqs, chunk), i16),
+            pltpu.VMEM((2, count, 2 * seqs, chunk), i16),
+            pltpu.VMEM((2, count, 2 * seqs, chunk // 2), i16),
+            pltpu.VMEM((2, count, 2 * seqs, chunk // 2), i16),
+            dma((SLOTS,)),
+            dma((2, 2, count)),
+            dma((2, 2, count)),
+            dma((2, 2, count)),
+            dma((2, 2, count)),
+            dma((2, 4)),
+            dma((2, 4)),
+            dma((2, 4)),
+            dma((2, count)),
+            dma((count // 2, 8)),
+            dma((2, count // 2)),
+            dma((2, 2, 4)),
+            dma((2, 8)),
+            dma((2, 5)),
+            dma((2, 2, 3, 4)),
+        ],
+        cost_estimate=pl.CostEstimate(flops=4 * total * rows * depth, bytes_accessed=4 * rows * depth, transcendentals=0),
+        compiler_params=pltpu.CompilerParams(collective_id=0, has_side_effects=True, vmem_limit_bytes=60 << 20),
+    )(hot1, hot0, emission, last, forward, transition)
+
+
+def final_kernel(fall_ref, zall_ref, gw_ref, win_ref, u_ref, back_ref, count_ref):
+    seqs = u_ref.shape[1]
+    c = lax.axis_index("col")
+
+    def work(h):
+        totals = None
+        for time in (1, 0):
+            parts = []
+            for src in range(8):
+                value = fall_ref[time, src].astype(jnp.float32)[h * seqs:(h + 1) * seqs]
+                parts.append(value * (1.0 / zall_ref[src, time, :, :1]))
+            weight = jnp.concatenate(parts, axis=0).astype(jnp.bfloat16)
+            term = lax.dot_general(weight, gw_ref[time], (((0,), (0,)), ((), ())), preferred_element_type=jnp.float32)
+            totals = term if totals is None else totals + term
+        count_ref[...] = win_ref[...].astype(jnp.float32) * totals * (H * H / N)
+
+    half = pl.program_id(1)
+    for h in range(2):
+        pl.when(half == h)(functools.partial(work, h))
+    for time in range(2):
+        back_ref[time] = u_ref[time] * (1.0 / zall_ref[c, time, :, :1])
+
+
+def final_call(forward_all, zall, picked, transition, u):
+    rows = transition.shape[0]
+    seqs = u.shape[1]
+    block = 512
+    tiles = rows // 2 // block
+    return pl.pallas_call(
+        final_kernel,
+        grid=(tiles, 2),
+        in_specs=[
+            pl.BlockSpec((2, 8, 2 * seqs, block), lambda j, h: (0, 0, 0, j)),
+            pl.BlockSpec(zall.shape, lambda j, h: (0, 0, 0, 0)),
+            pl.BlockSpec(picked.shape, lambda j, h: (0, 0, 0)),
+            pl.BlockSpec((block, DW), lambda j, h: (h * tiles + j, 0)),
+            pl.BlockSpec((2, seqs, block), lambda j, h: (0, 0, h * tiles + j)),
+        ],
+        out_specs=[
+            pl.BlockSpec((2, seqs, block), lambda j, h: (0, 0, h * tiles + j)),
+            pl.BlockSpec((block, DW), lambda j, h: (h * tiles + j, 0)),
+        ],
+        out_shape=[
+            jax.ShapeDtypeStruct(u.shape, jnp.float32),
+            jax.ShapeDtypeStruct((rows, DW), jnp.float32),
+        ],
+    )(forward_all, zall, picked, transition, u)
+
+
+def fast_device(transition, emission, token_ids, forward, backward_last):
+    row_index = lax.axis_index("row")
+    row_seqs = backward_last.shape[0]
+    seqs = forward.shape[1]
+    tokens = lax.dynamic_slice_in_dim(token_ids[1], row_index * row_seqs, row_seqs, 0)
+    hot1 = (tokens[:, None] == lax.broadcasted_iota(jnp.int32, (row_seqs, emission.shape[0]), 1)).astype(jnp.bfloat16)
+    hot0 = (token_ids[0][:, None] == lax.broadcasted_iota(jnp.int32, (8 * seqs, emission.shape[0]), 1)).astype(jnp.bfloat16)
+    u, zall, picked, forward_all = big_call(hot1, hot0, emission, backward_last, forward, transition)
+    backward, counts = final_call(forward_all, zall, picked, transition, u)
+    return (backward, counts)
 
 
 def in_order(arrived, index):
@@ -57,6 +605,21 @@
         got = lax.ppermute(piece, "col", [(c, (c + 2 * k) % col_count) for c in range(col_count)])
         total = total + got.astype(jnp.float32)
     return total
+
+
+def plain_product(weighted_back, transition, scale, scale_mine, col_count, col_index, local_seqs):
+    chunk = transition.shape[0] // CHUNKS
+    pieces = []
+    for k in range(CHUNKS):
+        rows = slice(k * chunk, (k + 1) * chunk)
+        partial = lax.dot_general(
+            weighted_back, transition[rows], (((1,), (1,)), ((), ())), preferred_element_type=jnp.float32
+        )
+        away, keep = split_pair(partial, scale, col_count, col_index, local_seqs)
+        if k < CHUNKS - 1:
+            weighted_back, away = lax.optimization_barrier((weighted_back, away))
+        pieces.append(reduce_scatter(away, keep, col_count, col_index))
+    return jnp.concatenate(pieces, axis=1) / scale_mine
 
 
 def on_device(transition, emission, token_ids, forward, backward_last):
@@ -78,7 +641,6 @@
     beta = backward_last
     scale = jnp.full((seq_total, 1), 64.0, jnp.float32)
     scale_mine = jnp.full((local_seqs, 1), 64.0, jnp.float32)
-    chunk = block_src // CHUNKS
     for step in (1, 0):
         tokens = lax.dynamic_slice_in_dim(token_ids[step], row_index * row_seqs, row_seqs, 0)
         onehot = (tokens[:, None] == columns).astype(jnp.bfloat16)
@@ -88,17 +650,7 @@
         picked[step] = weighted_back[:, :DW]
         if step == 1:
             forward_all = lax.all_gather(forward, "col", axis=1, tiled=True)
-        pieces = []
-        for k in range(CHUNKS):
-            rows = slice(k * chunk, (k + 1) * chunk)
-            partial = lax.dot_general(
-                weighted_back, transition[rows], (((1,), (1,)), ((), ())), preferred_element_type=jnp.float32
-            )
-            away, keep = split_pair(partial, scale, col_count, col_index, local_seqs)
-            if k < CHUNKS - 1:
-                weighted_back, away = lax.optimization_barrier((weighted_back, away))
-            pieces.append(reduce_scatter(away, keep, col_count, col_index))
-        mine = jnp.concatenate(pieces, axis=1) / scale_mine
+        mine = plain_product(weighted_back, transition, scale, scale_mine, col_count, col_index, local_seqs)
         norm = jnp.sum(forward[step].astype(jnp.float32) * mine, axis=1)
         sums = lax.psum(jnp.stack([norm, jnp.sum(mine, axis=1)]), "row")
         sums_all = gather_small(sums, col_count, col_index)
@@ -130,6 +682,7 @@
 def solution(mesh):
     in_specs = (P("row", "col"), P(None, "col"), P(), P(None, "col", "row"), P("row", "col"))
     out_specs = (P(None, "col", "row"), P("row", "col"))
+    fits = mesh.shape["row"] == 4 and mesh.shape["col"] == 8
     return jax.shard_map(
-        on_device, mesh=mesh, in_specs=in_specs, out_specs=out_specs, check_vma=False
+        fast_device if fits else on_device, mesh=mesh, in_specs=in_specs, out_specs=out_specs, check_vma=False
     )

time: 323 us -> 218 us (0.67)
  Pallas kernels: 0 us -> 215 us
  waiting for transfers between devices: 101 us -> 0 us
  starting transfers between devices: 99.3 us -> 0 us
  matrix products: 78.8 us -> 0 us
  between operations: 14.8 us -> 0.65 us
  other arithmetic: 14.3 us -> 1.39 us
  blocking collectives: 11.7 us -> 0 us
    pallas_call x0 -> x2, Pallas kernels: none -> 215 us  [the longest x1 199 us: big_call(): pl.pallas_call(functools.partial(big_kernel, codes), out_shape=(jax.Shape...]
    ppermute x36 -> x0, waiting for transfers between devices: 101 us -> none  [the longest x12 39.3 us: reduce_scatter(): lax.ppermute(piece, 'col', [(c, (c + 2 * k) % col_count) for c in range(c...]
    ppermute x36 -> x0, starting transfers between devices: 99.2 us -> none  [the longest x14 59.1 us: gather_small(): lax.ppermute(value, 'col', [(c, (c + k) % col_count) for c in range(col_c...]
    dot_general x8 -> x0, matrix products: 78.8 us -> none  [the longest x4 68.2 us: on_device(): lax.dot_general(weighted_back, transition[rows], (((1,), (1,)), ((), ()))...]
    psum x2 -> x0, blocking collectives: 11.7 us -> none  [on_device(): sums = lax.psum(jnp.stack([norm, jnp.sum(mine, axis=1)]), 'row')]
    convert_element_type x8 -> x2, other arithmetic: 7.55 us -> 1.39 us  [the longest x1 0.71 us: fast_device(): (token_ids[0][:, None] == lax.broadcasted_iota(jnp.int32, (8 * seqs, emis...]
    another operation x11 -> x0, other arithmetic: 4.04 us -> none  [the longest x4 1.53 us: gather_rows(): jnp.stack([jnp.where(even, own, got), jnp.where(even, got, own)], axis=1)]
  transfers between devices with their start and end apart: 37 -> 0, of which waited for: 14 -> 0; matrix products, arithmetic and copies ran while one was open for 26% -> 0% of each run, Pallas kernels for 0% -> 0%
where the time goes in v2:
time: 218 us
  Pallas kernels  215 us (99%)
    pallas_call x1, Pallas kernels, big_call(): pl.pallas_call(functools.partial(big_kernel, codes), out_shape=(jax.Shape...  199 us
    pallas_call x1, Pallas kernels, final_call(): pl.pallas_call(final_kernel, grid=(tiles, 2), in_specs=[pl.BlockSpec((2,...  15.9 us

profile of v2, /device:TPU:0, one launch (start us, length us, event | category | flops | bytes accessed | tf_op | source)
XLA Modules:
  0.0 218.0 jit_solution(3503212410382741759)
XLA Ops:
  0.6 0.8 fusion.2
  1.4 0.1 dynamic-slice_bitcast_fusion
  1.5 0.7 fusion.1.hot1_ref
  2.1 0.7 fusion.hot0_ref
  2.9 199.2 %shard_map.68 = (f32[2,24,8192]{2,1,0:T(8,128)}, f32[8,2,24,128]{3,2,1,0:T(8,128)}, bf16[2,192,128]{2,1,0:T(8,128)(2,1)}, bf16[2,8,48,4096]{3,2,1,0:T(8,128)(2,1)}) custom-call(bf16[48,96]{1,0:T(8,128)(2,1)} %fusion.1.hot1_ref, bf16[192,96]{1,0:T(8,128)(2,1)} %fusion.hot0_ref, bf16[96,4096]{1,0:T(8,128)(2,1)} %emit_ref.1, f32[48,4096]{1,0:T(8,128)} %last_ref.1, ...), custom_call_target="tpu_custom_call" | custom-call | flops 25769803776 | bytes 134217728 | tf_op jit(solution)/shard_map/pallas_call | solution.py:448
  202.1 15.9 %shard_map.69 = (f32[2,24,8192]{2,1,0:T(8,128)}, f32[8192,128]{1,0:T(8,128)}) custom-call(bf16[2,8,48,4096]{3,2,1,0:T(8,128)(2,1)} %get-tuple-element.6.fall_ref, f32[8,2,24,128]{3,2,1,0:T(8,128)} %get-tuple-element.7.zall_ref, bf16[2,192,128]{2,1,0:T(8,128)(2,1)} %get-tuple-element.8.gw_ref, bf16[8192,4096]{1,0:T(8,128)(2,1)} %win_ref.1, ...), custom_call_target="tpu_custom_call" | custom-call | tf_op jit(solution)/shard_map/pallas_call | solution.py:527

commit v3 on v2

--- a/solution.py
+++ b/solution.py
@@ -104,58 +104,79 @@
         g_move(r, j, gy_sem, r2).start()
         g_move(r, j, gc_sem, r1).start()
 
-    def fx_move(i, t, block):
-        at = fall_ref.at[t, block]
-        return remote(at, at, fx_sem.at[0, i], fx_sem.at[1, i], r, px)
-
-    def fz_move(way, kind, src, to):
+    bit = fall_ref.shape[3] // PIECES
+
+    def piece(t, block, p):
+        return fall_ref.at[t, block, :, pl.ds(pl.multiple_of(p * bit, bit), bit)]
+
+    def fx_move(i, t, block, p):
+        at = piece(t, block, p)
+        return remote(at, at, fx_sem.at[0, i, p], fx_sem.at[1, i, p], r, px)
+
+    def fz_move(way, kind, src, to, p):
         t = 0 if kind == 0 else 1
-        block = 2 * src + (x if kind < 2 else 1 - x)
-        at = fall_ref.at[t, block]
-        return remote(at, at, fz_sem.at[0, way, kind, src], fz_sem.at[1, way, kind, src], r, 2 * to + x)
-
-    def fz_send(kind, d):
+        at = piece(t, 2 * src + (x if kind < 2 else 1 - x), p)
+        return remote(at, at, fz_sem.at[0, way, kind, src, p], fz_sem.at[1, way, kind, src, p], r, 2 * to + x)
+
+    def fz_send(kind, d, p, act=lambda move: move.start()):
         @pl.when((z < 3) & (z - d + 1 >= 0))
         def _():
-            fz_move(0, kind, z - d + 1, z + 1).start()
+            act(fz_move(0, kind, z - d + 1, z + 1, p))
 
         @pl.when((z > 0) & (z + d - 1 <= 3))
         def _():
-            fz_move(1, kind, z + d - 1, z - 1).start()
-
-    def fz_sent(kind, d):
-        @pl.when((z < 3) & (z - d + 1 >= 0))
-        def _():
-            fz_move(0, kind, z - d + 1, z + 1).wait_send()
-
-        @pl.when((z > 0) & (z + d - 1 <= 3))
-        def _():
-            fz_move(1, kind, z + d - 1, z - 1).wait_send()
-
-    def fz_got(kind, d):
+            act(fz_move(1, kind, z + d - 1, z - 1, p))
+
+    def fz_got(kind, d, p):
         @pl.when(z - d >= 0)
         def _():
-            fz_move(0, kind, z - d, z).wait_recv()
+            fz_move(0, kind, z - d, z, p).wait_recv()
 
         @pl.when(z + d <= 3)
         def _():
-            fz_move(1, kind, z + d, z).wait_recv()
-
-    def fx_each(d, act):
+            fz_move(1, kind, z + d, z, p).wait_recv()
+
+    def fx_each(d, act, p):
         @pl.when(z - d >= 0)
         def _():
-            act(fx_move(1 + z - d, 0, 2 * (z - d) + x))
+            act(fx_move(1 + z - d, 0, 2 * (z - d) + x, p))
 
         if d:
             @pl.when(z + d <= 3)
             def _():
-                act(fx_move(1 + z + d, 0, 2 * (z + d) + x))
+                act(fx_move(1 + z + d, 0, 2 * (z + d) + x, p))
 
     def start(move):
         move.start()
 
-    fx_move(0, 1, c).start()
-    fz_send(0, 1)
+    def onward(kinds, d, p):
+        for kind in kinds:
+            if d > 1:
+                fz_got(kind, d - 1, p)
+            if d < 4:
+                fz_send(kind, d, p)
+
+    def pair_lines(p):
+        fx_move(0, 1, c, p).wait_recv()
+        onward((1, 2), 1, p)
+
+    acts = {
+        "pair": lambda p: fx_move(0, 1, c, p).start(), "one1": lambda p: onward((0,), 1, p),
+        "one2": lambda p: onward((0,), 2, p), "one3": lambda p: onward((0,), 3, p), "one4": lambda p: onward((0,), 4, p),
+        "two1": pair_lines, "two2": lambda p: onward((1, 2), 2, p), "two3": lambda p: onward((1, 2), 3, p),
+        "own": lambda p: fx_each(0, start, p), "near": lambda p: fx_each(1, start, p), "mid": lambda p: fx_each(2, start, p),
+        "far": lambda p: fx_each(3, start, p),
+    }
+
+    def whole(name):
+        def body(p, carry):
+            acts[name](p)
+            return carry
+
+        lax.fori_loop(0, PIECES, body, 0)
+
+    for name in PLAN:
+        whole(name)
     for j in range(4):
         g_move(r, j, gy_sem, r2).wait_recv()
         g_move(r2, j, gd_sem, r1).start()
@@ -163,36 +184,6 @@
         g_move(r, j, gc_sem, r1).wait()
         g_move(r2, j, gd_sem, r1).wait()
         g_move(r, j, gy_sem, r2).wait_send()
-    fx_each(0, start)
-    fx_move(0, 1, c).wait_recv()
-    fz_send(1, 1)
-    fz_send(2, 1)
-
-    def tick1a():
-        fz_got(0, 1)
-        fz_send(0, 2)
-
-    def tick1b():
-        for kind in (1, 2):
-            fz_got(kind, 1)
-            fz_send(kind, 2)
-
-    def tick1c():
-        fz_got(0, 2)
-        fz_send(0, 3)
-        fx_each(1, start)
-
-    def tick1d():
-        fx_each(2, start)
-
-    def tick0a():
-        for kind in (1, 2):
-            fz_got(kind, 2)
-            fz_send(kind, 3)
-
-    def tick0b():
-        fz_got(0, 3)
-        fx_each(3, start)
 
     def two(value):
         return jnp.concatenate([value[:, :half], value[:, half:]], axis=0)
@@ -246,8 +237,8 @@
                 x_move(m).start()
                 q_buf[lax.rem(m, deep)] = p_buf[:, x]
 
-            for at, act in ticks:
-                pl.when(m == at)(act)
+            for at, name in ticks:
+                pl.when((m >= at) & (m < at + PIECES))(functools.partial(acts[name], m - at))
 
             @pl.when((m >= LAG) & (m < count + LAG))
             def _():
@@ -383,13 +374,16 @@
         for d in range(1, 4):
             z_move(time, d).start()
 
-    run(0, g1, TICKS1(tick1a, tick1b, tick1c, tick1d))
+    run(0, g1, PLAN1)
     z_start(1)
-    run(1, g0, TICKS0(tick0a, tick0b))
+    run(1, g0, PLAN0)
     z_start(0)
     gw_ref[1] = g1[:, :, :128].reshape(8 * seqs, 128)
     gw_ref[0] = g0[:, :128]
-    for time in (1, 0):
+    def zc_move(time, d):
+        return remote(zc.at[time], zall_ref.at[c, time], zc_sem.at[0, time, d], zc_sem.at[1, time, d], r, lax.rem(c + d, 8))
+
+    def z_spread(time):
         for d in range(1, 4):
             z_move(time, d).wait()
         zr[time, 0] = zs[time]
@@ -398,25 +392,29 @@
             return zr[time, lax.rem(r + 4 - i, 4)]
 
         zc[time] = (arrived(0) + arrived(1)) + (arrived(2) + arrived(3))
-
-    def zc_move(d):
-        return remote(zc, zall_ref.at[c], zc_sem.at[0, d], zc_sem.at[1, d], r, lax.rem(c + d, 8))
-
-    for d in range(1, 8):
-        zc_move(d).start()
-    zall_ref[c] = zc[...]
-    fx_move(0, 1, c).wait_send()
-    for d in range(4):
-        fx_each(d, lambda move: move.wait_send())
-    for src in range(4):
-        fx_move(1 + src, 0, 2 * src + x).wait_recv()
-    for kind in range(3):
-        for d in (1, 2, 3):
-            fz_sent(kind, d)
-    for kind in (1, 2):
-        fz_got(kind, 3)
-    for d in range(1, 8):
-        zc_move(d).wait()
+        zall_ref[c, time] = zc[time]
+        for d in range(1, 8):
+            zc_move(time, d).start()
+
+    z_spread(1)
+    z_spread(0)
+    def finish(p, carry):
+        for kind in (1, 2):
+            fz_got(kind, 3, p)
+        for kind in range(3):
+            for d in (1, 2, 3):
+                fz_send(kind, d, p, lambda move: move.wait_send())
+        fx_move(0, 1, c, p).wait_send()
+        for d in range(4):
+            fx_each(d, lambda move: move.wait_send(), p)
+        for src in range(4):
+            fx_move(1 + src, 0, 2 * src + x, p).wait_recv()
+        return carry
+
+    lax.fori_loop(0, PIECES, finish, 0)
+    for time in range(2):
+        for d in range(1, 8):
+            zc_move(time, d).wait()
 
 
 LAG = 2
@@ -424,12 +422,10 @@
 GAP2 = 2
 
 
-def TICKS1(a, b, c, d):
-    return ((3, a), (10, b), (16, c), (21, d))
-
-
-def TICKS0(a, b):
-    return ((1, a), (6, b))
+PIECES = 8
+PLAN = ("pair", "one1")
+PLAN1 = ((1, "one2"), (8, "one3"), (14, "two1"), (14, "own"))
+PLAN0 = ((0, "one4"), (0, "two2"), (8, "near"), (8, "two3"), (16, "mid"), (16, "far"))
 
 
 def big_call(hot1, hot0, emission, last, forward, transition):
@@ -487,9 +483,9 @@
             dma((count // 2, 8)),
             dma((2, count // 2)),
             dma((2, 2, 4)),
-            dma((2, 8)),
-            dma((2, 5)),
-            dma((2, 2, 3, 4)),
+            dma((2, 2, 8)),
+            dma((2, 5, PIECES)),
+            dma((2, 2, 3, 4, PIECES)),
         ],
         cost_estimate=pl.CostEstimate(flops=4 * total * rows * depth, bytes_accessed=4 * rows * depth, transcendentals=0),
         compiler_params=pltpu.CompilerParams(collective_id=0, has_side_effects=True, vmem_limit_bytes=60 << 20),
@@ -501,15 +497,13 @@
     c = lax.axis_index("col")
 
     def work(h):
-        totals = None
-        for time in (1, 0):
-            parts = []
+        parts = []
+        for time in range(2):
             for src in range(8):
                 value = fall_ref[time, src].astype(jnp.float32)[h * seqs:(h + 1) * seqs]
                 parts.append(value * (1.0 / zall_ref[src, time, :, :1]))
-            weight = jnp.concatenate(parts, axis=0).astype(jnp.bfloat16)
-            term = lax.dot_general(weight, gw_ref[time], (((0,), (0,)), ((), ())), preferred_element_type=jnp.float32)
-            totals = term if totals is None else totals + term
+        weight = jnp.concatenate(parts, axis=0).astype(jnp.bfloat16)
+        totals = jnp.dot(gw_ref[...], weight, preferred_element_type=jnp.float32).T
         count_ref[...] = win_ref[...].astype(jnp.float32) * totals * (H * H / N)
 
     half = pl.program_id(1)
@@ -522,7 +516,7 @@
 def final_call(forward_all, zall, picked, transition, u):
     rows = transition.shape[0]
     seqs = u.shape[1]
-    block = 512
+    block = 2048
     tiles = rows // 2 // block
     return pl.pallas_call(
         final_kernel,
@@ -530,7 +524,7 @@
         in_specs=[
             pl.BlockSpec((2, 8, 2 * seqs, block), lambda j, h: (0, 0, 0, j)),
             pl.BlockSpec(zall.shape, lambda j, h: (0, 0, 0, 0)),
-            pl.BlockSpec(picked.shape, lambda j, h: (0, 0, 0)),
+            pl.BlockSpec(picked.shape, lambda j, h: (0, 0)),
             pl.BlockSpec((block, DW), lambda j, h: (h * tiles + j, 0)),
             pl.BlockSpec((2, seqs, block), lambda j, h: (0, 0, h * tiles + j)),
         ],
@@ -553,7 +547,7 @@
     hot1 = (tokens[:, None] == lax.broadcasted_iota(jnp.int32, (row_seqs, emission.shape[0]), 1)).astype(jnp.bfloat16)
     hot0 = (token_ids[0][:, None] == lax.broadcasted_iota(jnp.int32, (8 * seqs, emission.shape[0]), 1)).astype(jnp.bfloat16)
     u, zall, picked, forward_all = big_call(hot1, hot0, emission, backward_last, forward, transition)
-    backward, counts = final_call(forward_all, zall, picked, transition, u)
+    backward, counts = final_call(forward_all, zall, picked.reshape(16 * seqs, DW).T, transition, u)
     return (backward, counts)
 
 

time: 218 us -> 199 us (0.913)
  Pallas kernels: 215 us -> 195 us
    pallas_call x1, Pallas kernels: 199 us -> 186 us  [big_call(): pl.pallas_call(functools.partial(big_kernel, codes), out_shape=(jax.Shape...]
    pallas_call x1, Pallas kernels: 15.9 us -> 8.75 us  [final_call(): pl.pallas_call(final_kernel, grid=(tiles, 2), in_specs=[pl.BlockSpec((2,...]
where the time goes in v3:
time: 199 us
  Pallas kernels  195 us (98%)
  local copies, waits for them, and re-layouts  2.46 us (1%)
    pallas_call x1, Pallas kernels, big_call(): pl.pallas_call(functools.partial(big_kernel, codes), out_shape=(jax.Shape...  186 us
    pallas_call x1, Pallas kernels, final_call(): pl.pallas_call(final_kernel, grid=(tiles, 2), in_specs=[pl.BlockSpec((2,...  8.75 us

profile of v3, /device:TPU:0, one launch (start us, length us, event | category | flops | bytes accessed | tf_op | source)
XLA Modules:
  0.0 199.1 jit_solution(5017732957690594671)
XLA Ops:
  0.6 0.8 fusion.2
  1.4 0.1 dynamic-slice_bitcast_fusion
  1.5 0.7 fusion.1.hot1_ref
  2.1 0.7 fusion.hot0_ref
  2.9 185.9 %shard_map.68 = (f32[2,24,8192]{2,1,0:T(8,128)}, f32[8,2,24,128]{3,2,1,0:T(8,128)}, bf16[2,192,128]{2,1,0:T(8,128)(2,1)}, bf16[2,8,48,4096]{3,2,1,0:T(8,128)(2,1)}) custom-call(bf16[48,96]{1,0:T(8,128)(2,1)} %fusion.1.hot1_ref, bf16[192,96]{1,0:T(8,128)(2,1)} %fusion.hot0_ref, bf16[96,4096]{1,0:T(8,128)(2,1)} %emit_ref.1, f32[48,4096]{1,0:T(8,128)} %last_ref.1, ...), custom_call_target="tpu_custom_call" | custom-call | flops 25769803776 | bytes 134217728 | tf_op jit(solution)/shard_map/pallas_call | solution.py:444
  188.7 1.6 copy.8
  190.4 8.8 %shard_map.69 = (f32[2,24,8192]{2,1,0:T(8,128)}, f32[8192,128]{1,0:T(8,128)}) custom-call(bf16[2,8,48,4096]{3,2,1,0:T(8,128)(2,1)} %get-tuple-element.6.fall_ref, f32[8,2,24,128]{3,2,1,0:T(8,128)} %get-tuple-element.7.zall_ref, bf16[128,384]{1,0:T(8,128)(2,1)} %bitcast.5, bf16[8192,4096]{1,0:T(8,128)(2,1)} %win_ref.1, f32[2,24,8192]{2,1,0:T(8,128)} %get-tuple-element.9.u_ref), custom_call_target="tpu_custom_call" | custom-call | tf_op jit(solution)/shard_map/pallas_call | solution.py:521

commit v4 on v3

--- a/solution.py
+++ b/solution.py
@@ -424,8 +424,8 @@
 
 PIECES = 8
 PLAN = ("pair", "one1")
-PLAN1 = ((1, "one2"), (8, "one3"), (14, "two1"), (14, "own"))
-PLAN0 = ((0, "one4"), (0, "two2"), (8, "near"), (8, "two3"), (16, "mid"), (16, "far"))
+PLAN1 = ((0, "one2"), (5, "one3"), (14, "own"))
+PLAN0 = ((0, "one4"), (0, "two1"), (8, "two2"), (16, "near"), (16, "two3"), (16, "mid"), (16, "far"))
 
 
 def big_call(hot1, hot0, emission, last, forward, transition):

time: 199 us -> 188 us (0.945)
  Pallas kernels: 195 us -> 184 us
    pallas_call x1, Pallas kernels: 186 us -> 175 us  [big_call(): pl.pallas_call(functools.partial(big_kernel, codes), out_shape=(jax.Shape...]
where the time goes in v4:
time: 188 us
  Pallas kernels  184 us (98%)
  local copies, waits for them, and re-layouts  2.46 us (1%)
    pallas_call x1, Pallas kernels, big_call(): pl.pallas_call(functools.partial(big_kernel, codes), out_shape=(jax.Shape...  175 us
    pallas_call x1, Pallas kernels, final_call(): pl.pallas_call(final_kernel, grid=(tiles, 2), in_specs=[pl.BlockSpec((2,...  8.75 us

profile of v4, /device:TPU:0, one launch (start us, length us, event | category | flops | bytes accessed | tf_op | source)
XLA Modules:
  0.0 188.0 jit_solution(14465853634533858088)
XLA Ops:
  0.6 0.8 fusion.2
  1.4 0.1 dynamic-slice_bitcast_fusion
  1.5 0.7 fusion.1.hot1_ref
  2.1 0.7 fusion.hot0_ref
  2.9 174.8 %shard_map.68 = (f32[2,24,8192]{2,1,0:T(8,128)}, f32[8,2,24,128]{3,2,1,0:T(8,128)}, bf16[2,192,128]{2,1,0:T(8,128)(2,1)}, bf16[2,8,48,4096]{3,2,1,0:T(8,128)(2,1)}) custom-call(bf16[48,96]{1,0:T(8,128)(2,1)} %fusion.1.hot1_ref, bf16[192,96]{1,0:T(8,128)(2,1)} %fusion.hot0_ref, bf16[96,4096]{1,0:T(8,128)(2,1)} %emit_ref.1, f32[48,4096]{1,0:T(8,128)} %last_ref.1, ...), custom_call_target="tpu_custom_call" | custom-call | flops 25769803776 | bytes 134217728 | tf_op jit(solution)/shard_map/pallas_call | solution.py:444
  177.6 1.6 copy.8
  179.3 8.8 %shard_map.69 = (f32[2,24,8192]{2,1,0:T(8,128)}, f32[8192,128]{1,0:T(8,128)}) custom-call(bf16[2,8,48,4096]{3,2,1,0:T(8,128)(2,1)} %get-tuple-element.6.fall_ref, f32[8,2,24,128]{3,2,1,0:T(8,128)} %get-tuple-element.7.zall_ref, bf16[128,384]{1,0:T(8,128)(2,1)} %bitcast.5, bf16[8192,4096]{1,0:T(8,128)(2,1)} %win_ref.1, f32[2,24,8192]{2,1,0:T(8,128)} %get-tuple-element.9.u_ref), custom_call_target="tpu_custom_call" | custom-call | tf_op jit(solution)/shard_map/pallas_call | solution.py:521

commit v5 on v4

--- a/solution.py
+++ b/solution.py
@@ -353,7 +353,7 @@
         if ti == 0:
             steps += GAP + GAP2
         lax.fori_loop(0, steps, body, 0)
-        if ti == 0:
+        if ti == 1:
             def sent(n, carry):
                 h = n % 2
                 for yy in range(2):

time: 188 us -> 188 us (level)
  no operation moved by 1% of the time
where the time goes in v5:
time: 188 us
  Pallas kernels  184 us (98%)
  local copies, waits for them, and re-layouts  2.46 us (1%)
    pallas_call x1, Pallas kernels, big_call(): pl.pallas_call(functools.partial(big_kernel, codes), out_shape=(jax.Shape...  175 us
    pallas_call x1, Pallas kernels, final_call(): pl.pallas_call(final_kernel, grid=(tiles, 2), in_specs=[pl.BlockSpec((2,...  8.76 us

profile of v5, /device:TPU:0, one launch (start us, length us, event | category | flops | bytes accessed | tf_op | source)
XLA Modules:
  0.0 188.0 jit_solution(579155950002695806)
XLA Ops:
  0.6 0.8 fusion.2
  1.4 0.1 dynamic-slice_bitcast_fusion
  1.5 0.7 fusion.1.hot1_ref
  2.1 0.7 fusion.hot0_ref
  2.9 174.8 %shard_map.68 = (f32[2,24,8192]{2,1,0:T(8,128)}, f32[8,2,24,128]{3,2,1,0:T(8,128)}, bf16[2,192,128]{2,1,0:T(8,128)(2,1)}, bf16[2,8,48,4096]{3,2,1,0:T(8,128)(2,1)}) custom-call(bf16[48,96]{1,0:T(8,128)(2,1)} %fusion.1.hot1_ref, bf16[192,96]{1,0:T(8,128)(2,1)} %fusion.hot0_ref, bf16[96,4096]{1,0:T(8,128)(2,1)} %emit_ref.1, f32[48,4096]{1,0:T(8,128)} %last_ref.1, ...), custom_call_target="tpu_custom_call" | custom-call | flops 25769803776 | bytes 134217728 | tf_op jit(solution)/shard_map/pallas_call | solution.py:444
  177.6 1.6 copy.8
  179.3 8.8 %shard_map.69 = (f32[2,24,8192]{2,1,0:T(8,128)}, f32[8192,128]{1,0:T(8,128)}) custom-call(bf16[2,8,48,4096]{3,2,1,0:T(8,128)(2,1)} %get-tuple-element.6.fall_ref, f32[8,2,24,128]{3,2,1,0:T(8,128)} %get-tuple-element.7.zall_ref, bf16[128,384]{1,0:T(8,128)(2,1)} %bitcast.5, bf16[8192,4096]{1,0:T(8,128)(2,1)} %win_ref.1, f32[2,24,8192]{2,1,0:T(8,128)} %get-tuple-element.9.u_ref), custom_call_target="tpu_custom_call" | custom-call | tf_op jit(solution)/shard_map/pallas_call | solution.py:521
